TPU v7x, 512 devices: a whole 4x8x8 slice. The times are simulated.
512 devices in a mesh: blk: 16 (over z_lo, x, core), dp: 32 (over z_hi, y).
Axes of the slice: x: 4, y: 8, z: 8 (z_hi: 4, z_lo: 2; z = z_hi * 2 + z_lo), core: 2. Of those that a mesh axis runs over, the one named last changes fastest.
Arguments:
- queries: bfloat16 [65536, 1024], P(('blk', 'dp')), may hold values from -0.5 to 0.5, as said below
- passages: bfloat16 [65536, 1024], P(('blk', 'dp')), may hold values from -0.5 to 0.5, as said below
- positive: int32 [65536], P(('blk', 'dp')), may hold values from 0 to 2047, as said below
- hard_ids: int32 [65536, 4], P(('blk', 'dp')), may hold values from 0 to 4095, as said below
- hard_count: int32 [65536], P(('blk', 'dp')), may hold values from 1 to 4
Outputs:
- query_grads: bfloat16 [65536, 1024], P(('blk', 'dp'))
- passage_grads: bfloat16 [65536, 1024], P(('blk', 'dp'))
Inputs may be any that keep to these rules, and one draw needn't show every extreme that they name: `queries`: encoder outputs. `passages`: encoder outputs. `positive`: index into the query's in-batch group. `hard_ids`: entry e names row e % 128 of the device with the query's blk index and dp index e // 128; among the rows of one device, at most 32 entries name one dp index, and exactly 32 entries name some dp index.
All inputs are finite; a program needn't handle non-finite values.
Results may differ from a plain program's by a relative error of at most 0.0079.
Values may be sent and summed in bfloat16 or wider, within the bound.
No kernel may reach another device: no remote copies, remote signals or barrier semaphores. Data moves between devices by JAX's collectives and lax.ppermute only.
A program may use at most 64 MiB of HBM per device.

v0:
```python
import jax
import jax.numpy as jnp
from jax import lax
from jax.experimental import pallas as pl
from jax.experimental.pallas import tpu as pltpu
from jax.sharding import PartitionSpec as P

EPS = 1e-06
TAU = 0.02


def unit_rows(x):
    xf = x.astype(jnp.float32)
    scale = lax.rsqrt(jnp.sum(xf * xf, axis=1, keepdims=True) + EPS)
    return (xf * scale, scale)


def unit_kernel(q_ref, p_ref, q_half, p_half, both, q_scale, p_scale):
    for at, x_ref, half, scale in ((0, p_ref, p_half, p_scale), (1, q_ref, q_half, q_scale)):
        unit, factor = unit_rows(x_ref[...])
        half[...] = unit.astype(jnp.bfloat16)
        both[at] = unit.astype(jnp.bfloat16)
        scale[...] = factor


def unit_halves(queries, passages):
    rows, width = queries.shape
    half = jax.ShapeDtypeStruct((rows, width), jnp.bfloat16)
    scale = jax.ShapeDtypeStruct((rows, 1), jnp.float32)
    return pl.pallas_call(
        unit_kernel,
        out_shape=(half, half, jax.ShapeDtypeStruct((2, rows, width), jnp.bfloat16), scale, scale),
        cost_estimate=pl.CostEstimate(
            flops=8 * rows * width, bytes_accessed=12 * rows * width, transcendentals=0
        ),
        name="unit_halves",
    )(queries, passages)


def pick_kernel(index_ref, pool_ref, out_ref):
    rows = pool_ref.shape[1]
    index = index_ref[0]
    pick = index == lax.broadcasted_iota(jnp.int32, (rows, index.shape[1]), 0)
    found = lax.dot_general(
        pick.astype(jnp.bfloat16),
        pool_ref[0],
        (((0,), (0,)), ((), ())),
        preferred_element_type=jnp.float32,
    )
    out_ref[...] = found.astype(jnp.bfloat16).reshape(out_ref.shape)


def pick_rows(index, pool):
    groups, rows, width = pool.shape
    _, parts, ranks = index.shape
    found = pl.pallas_call(
        pick_kernel,
        grid=(groups,),
        in_specs=[
            pl.BlockSpec((1, 1, parts * ranks), lambda g: (g, 0, 0)),
            pl.BlockSpec((1, rows, width), lambda g: (g, 0, 0)),
        ],
        out_specs=pl.BlockSpec((parts, 1, ranks, width), lambda g: (0, g, 0, 0)),
        out_shape=jax.ShapeDtypeStruct((parts, groups, ranks, width), jnp.bfloat16),
        compiler_params=room(4),
        cost_estimate=pl.CostEstimate(
            flops=2 * groups * rows * parts * ranks * width,
            bytes_accessed=2 * groups * (rows + parts * ranks) * width,
            transcendentals=0,
        ),
        name="pick_rows",
    )(index.reshape(groups, 1, parts * ranks), pool)
    return found.reshape(parts, groups * ranks, width)


TILE = 256


def room(mib):
    return pltpu.CompilerParams(vmem_limit_bytes=mib * 1024 * 1024)


def cost(rows, width, columns, exps=0):
    return pl.CostEstimate(
        flops=2 * rows * width * columns,
        bytes_accessed=2 * (rows + columns) * width + 4 * rows * columns,
        transcendentals=exps,
    )


def exp_kernel(x_ref, own_ref, other_ref, exp_ref, sum_ref):
    half = own_ref.shape[0]
    x = x_ref[...]
    added = jnp.zeros(sum_ref.shape, jnp.float32)
    for at, rows_ref in ((0, own_ref), (half, other_ref)):
        for tile in range(0, half, TILE):
            exps = jnp.exp(dot(x, rows_ref[tile : tile + TILE], 1, 1) / TAU)
            exp_ref[:, at + tile : at + tile + TILE] = exps
            added += jnp.sum(exps, axis=1, keepdims=True)
    sum_ref[...] = added


def exp_scores_of(x, own, other):
    rows = x.shape[0]
    return pl.pallas_call(
        exp_kernel,
        out_shape=(
            jax.ShapeDtypeStruct((rows, 2 * own.shape[0]), jnp.float32),
            jax.ShapeDtypeStruct((rows, 1), jnp.float32),
        ),
        compiler_params=room(8),
        cost_estimate=cost(rows, x.shape[1], 2 * own.shape[0], 2 * rows * own.shape[0]),
        name="exp_scores",
    )(x, own, other)


def total_kernel(q_ref, hard_ref, mask_ref, sum_ref, positive_ref, total_ref, w_ref, s_ref, facts_ref):
    rows = q_ref.shape[0]
    q = q_ref[...]
    exps = []
    total = sum_ref[...]
    for tile in range(0, hard_ref.shape[0], TILE):
        scores = dot(q, hard_ref[tile : tile + TILE], 1, 1) / TAU
        exps.append(jnp.where(mask_ref[:, tile : tile + TILE] > 0, jnp.exp(scores), 0.0))
        total += jnp.sum(exps[-1], axis=1, keepdims=True)
    total_ref[...] = total
    for number, exp_hard in enumerate(exps):
        tile = number * TILE
        weights = (exp_hard / total).astype(jnp.bfloat16)
        w_ref[:, tile : tile + TILE] = weights
        s_ref[:, tile : tile + TILE] = jnp.sum(weights.astype(jnp.float32), axis=0, keepdims=True)
    across = lax.broadcasted_iota(jnp.int32, (rows, rows), 0)
    down = lax.broadcasted_iota(jnp.int32, (rows, rows), 1)
    total_row = jnp.sum(jnp.where(across == down, total, 0.0), axis=0, keepdims=True)
    for device in range(facts_ref.shape[0]):
        facts_ref[device, 0:1] = total_row
        facts_ref[device, 1:2] = positive_ref[...].astype(jnp.float32)


def totals_of(q_half, hard_rows, mask, sums, positive, length):
    rows = q_half.shape[0]
    slots = hard_rows.shape[0]
    return pl.pallas_call(
        total_kernel,
        out_shape=(
            jax.ShapeDtypeStruct((rows, 1), jnp.float32),
            jax.ShapeDtypeStruct((rows, slots), jnp.bfloat16),
            jax.ShapeDtypeStruct((1, slots), jnp.float32),
            jax.ShapeDtypeStruct((length, 2, rows), jnp.float32),
        ),
        compiler_params=room(8),
        cost_estimate=cost(rows, q_half.shape[1], slots, rows * slots),
        name="totals",
    )(q_half, hard_rows, mask, sums, positive.reshape(1, rows))


def grad_kernel(exp_ref, total_ref, mark_ref, marks_ref, own, other, w_ref, x_ref, scale_ref, *rest):
    *chunks, out_ref, hard, sems = rest
    copies = []
    at = 0
    for number, chunk in enumerate(chunks):
        place = hard.at[pl.ds(at, chunk.shape[0])]
        copies.append(pltpu.make_async_copy(chunk, place, sems.at[number]))
        copies[-1].start()
        at += chunk.shape[0]
    half = own.shape[0]
    width = x_ref.shape[1]
    target = (mark_ref[...] == marks_ref[...]).astype(jnp.float32)
    grads = (exp_ref[...] / total_ref[...] - target).astype(jnp.bfloat16)
    weights = w_ref[...]
    scale = scale_ref[...]
    directions = []
    for tile in range(0, width, TILE):
        cols = slice(tile, tile + TILE)
        direction = dot(grads[:, :half], own[:, cols], 1, 0)
        directions.append(direction + dot(grads[:, half:], other[:, cols], 1, 0))
    for copy in copies:
        copy.wait()
    along = jnp.zeros(scale.shape, jnp.float32)
    for number in range(len(directions)):
        cols = slice(number * TILE, (number + 1) * TILE)
        direction = (directions[number] + dot(weights, hard[:, cols], 1, 0)) / TAU
        unit = x_ref[:, cols].astype(jnp.float32) * scale
        along += jnp.sum(unit * direction, axis=1, keepdims=True)
        directions[number] = direction
    for number, direction in enumerate(directions):
        cols = slice(number * TILE, (number + 1) * TILE)
        unit = x_ref[:, cols].astype(jnp.float32) * scale
        out_ref[:, cols] = (scale * (direction - unit * along)).astype(jnp.bfloat16)


def grads_of(exps, total, mark, marks, own, other, weights, hard, x, scale):
    operands = (exps, total, mark, marks, own, other, weights, x, scale)
    whole = pl.BlockSpec(memory_space=pltpu.VMEM)
    return pl.pallas_call(
        grad_kernel,
        in_specs=[whole] * len(operands) + [pl.BlockSpec(memory_space=pl.ANY)] * len(hard),
        out_specs=whole,
        out_shape=jax.ShapeDtypeStruct(x.shape, jnp.bfloat16),
        scratch_shapes=[
            pltpu.VMEM((weights.shape[1], x.shape[1]), jnp.bfloat16),
            pltpu.SemaphoreType.DMA((len(hard),)),
        ],
        compiler_params=room(12),
        cost_estimate=cost(*x.shape, exps.shape[1] + weights.shape[1]),
        name="gradients",
    )(*operands, *hard)


def dot(a, b, ca, cb):
    return lax.dot_general(a, b, (((ca,), (cb,)), ((), ())), preferred_element_type=jnp.float32)


def exchange(value, axis, groups=None):
    return lax.all_to_all(
        value, axis, split_axis=0, concat_axis=0, tiled=True, axis_index_groups=groups
    )


def shifted(value, axis, move):
    devices = lax.axis_size(axis)
    return lax.ppermute(value, axis, [(i, move(i)) for i in range(devices)])


def beside(i, step, length):
    half = length // 2
    return i // half * half + (i % half // 2 + step) % (half // 2) * 2 + i % 2


def sibling(i):
    return i // 2 * 2 + 1 - i % 2


def blk_order(me):
    length = lax.axis_size("blk")
    where = []
    for core in range(2):
        for step in range(length // 4):
            for z in range(2):
                there = beside((me + length // 2 * z) % length, -step, length)
                where.append(there // 2 * 2 + (there + core) % 2)
    return jnp.stack(where)


def gather_chips(both, after):
    length = lax.axis_size("blk")

    def turned(value, step):
        return shifted(value, "blk", lambda i: beside(i, step, length))

    over = shifted(both, "blk", lambda i: (i + length // 2) % length)
    over, after = lax.optimization_barrier((over, after))
    pair = jnp.stack([both, over])
    right = turned(pair, 1)
    left = turned(pair, -1)
    far = (turned(right[0], 1), turned(left[1], -1))
    blocks = (both, over, right[0], right[1], far[0], far[1], left[0], left[1])
    return [jnp.concatenate([block[k] for block in blocks]) for k in range(2)], after


def local(queries, passages, positive, hard_ids, hard_count):
    rows, width = queries.shape
    hmax = hard_ids.shape[1]
    length = lax.axis_size("blk")
    peers = lax.axis_size("dp")
    me_blk = lax.axis_index("blk")
    me_dp = lax.axis_index("dp")
    nz = 4
    ny = peers // nz
    me_z = me_dp // ny
    me_y = me_dp % ny
    limit = 2 * rows * hmax // peers
    slots = peers * limit
    entries = rows * hmax
    bf16 = jnp.bfloat16

    own_ids = hard_ids.T.reshape(entries)

    q_half, p_half, both, q_scale, p_scale = unit_halves(queries, passages)

    lines = [[z * ny + y for y in range(ny)] for z in range(nz)]
    line_ids = exchange(jnp.broadcast_to(own_ids[None, :], (ny, entries)), "dp", lines)
    q_line = lax.all_gather(q_half, "dp", axis=0, tiled=True, axis_index_groups=lines)

    def along_z(i, step):
        return (i + step * ny) % peers

    p_line = [p_half]
    p_line += [shifted(p_half, "dp", lambda i, t=t: along_z(i, -t)) for t in range(1, nz)]
    p_line = jnp.stack(p_line)

    number = jnp.arange(entries, dtype=jnp.int32)
    ranks = jnp.arange(limit, dtype=jnp.int32)
    turn = jnp.arange(nz, dtype=jnp.int32)
    earlier = (number[:, None] < number[None, :]).astype(bf16)

    coded = (line_ids % rows + 1) * (2 * rows) + (number % rows + 1)[None, :]
    owners = ((me_z + turn) % nz * ny + me_y)[:, None, None]
    mine = line_ids[None] // rows == owners
    count = dot(mine.astype(bf16).reshape(-1, entries), earlier, 1, 0).astype(jnp.int32)
    rank = jnp.where(mine, count.reshape(mine.shape), -1)
    hit = rank[:, :, None, :] == ranks[:, None]
    table = jnp.sum(jnp.where(hit, coded[None, :, None, :], 0), axis=-1)
    asked_row = table // (2 * rows) - 1
    asked_by = table % (2 * rows) - 1

    sent_p = pick_rows(asked_row, p_line)
    got_p = exchange(sent_p, "dp", lines).reshape(slots, width)

    sent_q = pick_rows(jnp.swapaxes(asked_by, 0, 1), q_line.reshape(ny, rows, width))
    (p_own, q_own), sent_q = gather_chips(both, sent_q)
    got_q = [sent_q[0]]
    got_q += [shifted(sent_q[t], "dp", lambda i, t=t: along_z(i, t)) for t in range(1, nz)]

    p_own, got_q[1] = lax.optimization_barrier((p_own, got_q[1]))
    q_own, got_q[2], got_q[3] = lax.optimization_barrier((q_own, got_q[2], got_q[3]))
    p_other = shifted(p_own, "blk", sibling)
    q_other = shifted(q_own, "blk", sibling)
    where = blk_order(me_blk)

    owner = own_ids // rows
    before = (owner[:, None] == owner[None, :]) & (number[None, :] < number[:, None])
    rank = jnp.sum(before.astype(jnp.int32), axis=1)
    step = owner % ny * nz + (owner // ny - me_z) % nz
    place = (step * limit + rank).reshape(hmax, rows)
    used = jnp.arange(hmax, dtype=jnp.int32)[:, None] < hard_count[None, :]
    used_place = jnp.where(used, place, -1)
    slot = jnp.arange(slots, dtype=jnp.int32)
    weighs = jnp.any(used_place[:, :, None] == slot[None, None, :], axis=0)
    wanted = jnp.where(used, own_ids.reshape(hmax, rows) % rows, 0)[:, :, None]
    own_asked = jnp.sum(
        jnp.where(used_place[:, :, None] == slot[None, None, :], wanted, 0), axis=(0, 1)
    )

    exp_scores, sums = exp_scores_of(q_half, p_own, p_other)
    sums, q_other = lax.optimization_barrier((sums, q_other))
    exp_back, _ = exp_scores_of(p_half, q_own, q_other)
    total, weights, slot_weights, facts = totals_of(
        q_half, got_p, weighs.astype(jnp.float32), sums, positive, length
    )

    peer = jnp.arange(peers, dtype=jnp.int32)
    step_of = (me_z + peer % nz) % nz * ny + peer // nz
    by_slot = jnp.stack([slot_weights[0], own_asked.astype(jnp.float32)])
    by_slot = by_slot.reshape(2, 1, peers, limit)
    to_owner = peer[:, None] == step_of[None, :]
    by_owner = jnp.sum(jnp.where(to_owner[None, :, :, None], by_slot, 0.0), axis=2)
    facts = exchange(facts, "blk")
    facts, by_owner, exp_scores, total = lax.optimization_barrier(
        (facts, by_owner, exp_scores, total)
    )
    got = exchange(jnp.swapaxes(by_owner, 0, 1), "dp")
    from_z = ((me_z - turn) % nz)[:, None] == turn[None, :]
    got = got.reshape(1, nz, ny, 2, limit)
    got = jnp.sum(jnp.where(from_z[:, :, None, None, None], got, 0.0), axis=1)
    got_weights = got[:, :, 0].reshape(1, slots)
    asked = got[:, :, 1].reshape(1, slots).astype(jnp.int32)
    names = asked == jnp.arange(rows, dtype=jnp.int32)[:, None]
    hard_back = jnp.where(names, got_weights, 0.0).astype(bf16)
    facts = facts[where]
    all_total = facts[:, 0].reshape(1, length * rows)
    all_positive = facts[:, 1].reshape(1, length * rows).astype(jnp.int32)

    row = jnp.arange(rows, dtype=jnp.int32)
    column = (where[:, None] * rows + row[None, :]).reshape(1, length * rows)
    own_row = me_blk * rows + row[:, None]
    query_grads = grads_of(
        exp_scores, total, positive[:, None], column,
        p_own, p_other, weights, [got_p], queries, q_scale,
    )
    passage_grads = grads_of(
        exp_back, all_total, own_row, all_positive,
        q_own, q_other, hard_back, got_q, passages, p_scale,
    )
    return (query_grads, passage_grads)


def solution(mesh):
    return jax.shard_map(
        local,
        mesh=mesh,
        in_specs=(
            P(("blk", "dp"), None),
            P(("blk", "dp"), None),
            P(("blk", "dp")),
            P(("blk", "dp"), None),
            P(("blk", "dp")),
        ),
        out_specs=(P(("blk", "dp"), None), P(("blk", "dp"), None)),
        check_vma=False,
    )
```

profile of v0, /device:TPU:2, one launch (start us, length us, event | category | flops | bytes accessed | tf_op | source)
XLA Modules:
  0.0 208.8 jit_solution(6915698643923565947)
XLA Ops:
  7.2 2.2 %unit_halves.1 = (bf16[128,1024]{1,0:T(8,128)(2,1)}, bf16[128,1024]{1,0:T(8,128)(2,1)}, bf16[2,128,1024]{2,1,0:T(8,128)(2,1)}, f32[128,1]{1,0:T(8,128)}, f32[128,1]{1,0:T(8,128)}) custom-call(bf16[128,1024]{1,0:T(8,128)(2,1)} %x_ref.2, bf16[128,1024]{1,0:T(8,128)(2,1)} %x_ref.3), custom_call_target="tpu_custom_call" | custom-call | flops 1048576 | bytes 1572864 | tf_op jit(solution)/shard_map/unit_halves/pallas_call | solution.py:30
  9.4 6.1 %collective-permute-start.2 = (bf16[128,1024]{1,0:T(8,128)(2,1)}, bf16[128,1024]{1,0:T(8,128)(2,1)S(1)}, u32[]{:S(2)}, u32[]{:S(2)}) collective-permute-start(bf16[128,1024]{1,0:T(8,128)(2,1)} %get-tuple-element.28.x_ref), channel_id=1, source_target_pairs={{0,8},{1,9},{2,10},{3,11},{4,12},{5,13},{6,14},{7,15},{8,16},{9,17... | collective-permute-start | bytes 786440 | tf_op jit(solution)/shard_map/ppermute | solution.py:222
  15.5 9.1 %collective-permute-start.1 = (bf16[128,1024]{1,0:T(8,128)(2,1)}, bf16[128,1024]{1,0:T(8,128)(2,1)S(1)}, u32[]{:S(2)}, u32[]{:S(2)}) collective-permute-start(bf16[128,1024]{1,0:T(8,128)(2,1)} %get-tuple-element.28.x_ref), channel_id=1, source_target_pairs={{0,16},{1,17},{2,18},{3,19},{4,20},{5,21},{6,22},{7,23},{8,24},{9,... | collective-permute-start | bytes 786440 | tf_op jit(solution)/shard_map/ppermute | solution.py:222
  24.6 3.7 %collective-permute-start = (bf16[128,1024]{1,0:T(8,128)(2,1)}, bf16[128,1024]{1,0:T(8,128)(2,1)S(1)}, u32[]{:S(2)}, u32[]{:S(2)}) collective-permute-start(bf16[128,1024]{1,0:T(8,128)(2,1)} %get-tuple-element.28.x_ref), channel_id=1, source_target_pairs={{0,24},{1,25},{2,26},{3,27},{4,28},{5,29},{6,30},{7,31},{8,0},{9,1... | collective-permute-start | bytes 786440 | tf_op jit(solution)/shard_map/ppermute | solution.py:222
  28.3 1.3 broadcast_in_dim.129
  29.6 7.1 %all-to-all-start = ((s32[8,1,512]{2,1,0:T(1,128)}), s32[8,1,512]{2,1,0:T(1,128)S(1)}, u32[]{:S(2)}, u32[]{:S(2)}) async-start(s32[8,1,512]{2,1,0:T(1,128)} %broadcast_in_dim.129), calls=%async_computation | async-start | bytes 32768 | tf_op jit(solution)/shard_map/all_to_all | solution.py:215
  36.7 3.4 %collective-permute-start.3 = (bf16[2,128,1024]{2,1,0:T(8,128)(2,1)}, bf16[2,128,1024]{2,1,0:T(8,128)(2,1)S(1)}, u32[]{:S(2)}, u32[]{:S(2)}) collective-permute-start(bf16[2,128,1024]{2,1,0:T(8,128)(2,1)} %get-tuple-element.29), channel_id=1, source_target_pairs={{0,256},{32,288},{64,320},{96,352},{128,384},{160,416},{192,448},{... | collective-permute-start | bytes 1572872 | tf_op jit(solution)/shard_map/ppermute | solution.py:222
  40.8 1.9 bitcast_dynamic-update-slice_fusion.1
  42.8 1.7 all-to-all-done
  45.6 13.2 %all-gather.2.cloned.1.call-done = bf16[1024,1024]{1,0:T(8,128)(2,1)} async-done(((bf16[128,1024]{1,0:T(8,128)(2,1)}), bf16[1024,1024]{1,0:T(8,128)(2,1)}) %all-gather.2.cloned.1.call-update) | async-done | bytes 2097168 | tf_op jit(solution)/shard_map/all_gather | solution.py:283
  58.7 1.6 copy-done.3
  60.3 2.2 %pick_rows.3 = bf16[4,8,32,1024]{3,2,1,0:T(8,128)(2,1)S(1)} custom-call(s32[8,1,128]{2,1,0:T(1,128)S(1)} %reshape.1216.index_ref, bf16[8,128,1024]{2,1,0:T(8,128)(2,1)S(1)} %bitcast.201), custom_call_target="tpu_custom_call" | custom-call | flops 268435456 | bytes 4194304 | tf_op jit(solution)/shard_map/pick_rows/pallas_call | solution.py:56
  62.5 1.3 copy-done
  63.9 1.1 pad_maximum_fusion.1
  64.9 3.4 %collective-permute-start.4 = (bf16[2,2,128,1024]{3,2,1,0:T(8,128)(2,1)}, bf16[2,2,128,1024]{3,2,1,0:T(8,128)(2,1)}, u32[]{:S(2)}, u32[]{:S(2)}) collective-permute-start(bf16[2,2,128,1024]{3,2,1,0:T(8,128)(2,1)} %pad_maximum_fusion.1), channel_id=1, source_target_pairs={{0,64},{32,96},{64,128},{96,160},{128,192},{160,224},{192,0},{224,... | collective-permute-start | bytes 3145736 | tf_op jit(solution)/shard_map/ppermute | solution.py:222
  69.1 2.5 %collective-permute-start.6 = (bf16[2,2,128,1024]{3,2,1,0:T(8,128)(2,1)}, bf16[2,2,128,1024]{3,2,1,0:T(8,128)(2,1)}, u32[]{:S(2)}, u32[]{:S(2)}) collective-permute-start(bf16[2,2,128,1024]{3,2,1,0:T(8,128)(2,1)} %pad_maximum_fusion.1), channel_id=1, source_target_pairs={{0,192},{32,224},{64,0},{96,32},{128,64},{160,96},{192,128},{224,1... | collective-permute-start | bytes 3145736 | tf_op jit(solution)/shard_map/ppermute | solution.py:222
  71.8 1.4 pick_rows.2
  73.3 1.3 copy-done.1
  74.6 4.8 %all-to-all-start.1 = ((bf16[8,128,1024]{2,1,0:T(8,128)(2,1)}), bf16[8,128,1024]{2,1,0:T(8,128)(2,1)S(1)}, u32[]{:S(2)}, u32[]{:S(2)}) async-start(bf16[8,128,1024]{2,1,0:T(8,128)(2,1)} %bitcast.200), calls=%async_computation.1 | async-start | bytes 4194304 | tf_op jit(solution)/shard_map/all_to_all | solution.py:215
  79.4 1.8 slice_bitcast_fusion.2
  81.2 4.4 %collective-permute-start.8 = (bf16[256,1024]{1,0:T(8,128)(2,1)S(1)}, bf16[256,1024]{1,0:T(8,128)(2,1)S(1)}, u32[]{:S(2)}, u32[]{:S(2)}) collective-permute-start(bf16[256,1024]{1,0:T(8,128)(2,1)S(1)} %get-tuple-element.55), channel_id=1, source_target_pairs={{0,8},{1,9},{2,10},{3,11},{4,12},{5,13},{6,14},{7,15},{8,16},{9,17... | collective-permute-start | bytes 1572872 | tf_op jit(solution)/shard_map/ppermute | solution.py:222
  85.6 5.8 %collective-permute-start.10 = (bf16[256,1024]{1,0:T(8,128)(2,1)S(1)}, bf16[256,1024]{1,0:T(8,128)(2,1)S(1)}, u32[]{:S(2)}, u32[]{:S(2)}) collective-permute-start(bf16[256,1024]{1,0:T(8,128)(2,1)S(1)} %get-tuple-element.54), channel_id=1, source_target_pairs={{0,16},{1,17},{2,18},{3,19},{4,20},{5,21},{6,22},{7,23},{8,24},{9,... | collective-permute-start | bytes 1572872 | tf_op jit(solution)/shard_map/ppermute | solution.py:222
  91.5 5.6 %collective-permute-start.11 = (bf16[256,1024]{1,0:T(8,128)(2,1)S(1)}, bf16[256,1024]{1,0:T(8,128)(2,1)S(1)}, u32[]{:S(2)}, u32[]{:S(2)}) collective-permute-start(bf16[256,1024]{1,0:T(8,128)(2,1)S(1)} %get-tuple-element.53), channel_id=1, source_target_pairs={{0,24},{1,25},{2,26},{3,27},{4,28},{5,29},{6,30},{7,31},{8,0},{9,1... | collective-permute-start | bytes 1572872 | tf_op jit(solution)/shard_map/ppermute | solution.py:222
  97.1 0.8 bitcast_dynamic-update-slice_fusion
  97.9 1.1 slice_bitcast_fusion.1
  99.0 3.4 %collective-permute-start.5 = (bf16[2,128,1024]{2,1,0:T(8,128)(2,1)S(1)}, bf16[2,128,1024]{2,1,0:T(8,128)(2,1)S(1)}, u32[]{:S(2)}, u32[]{:S(2)}) collective-permute-start(bf16[2,128,1024]{2,1,0:T(8,128)(2,1)S(1)} %slice_bitcast_fusion.1), channel_id=1, source_target_pairs={{0,64},{32,96},{64,128},{96,160},{128,192},{160,224},{192,0},{224,... | collective-permute-start | bytes 1572872 | tf_op jit(solution)/shard_map/ppermute | solution.py:222
  102.4 1.1 slice_bitcast_fusion
  103.5 2.5 %collective-permute-start.7 = (bf16[2,128,1024]{2,1,0:T(8,128)(2,1)S(1)}, bf16[2,128,1024]{2,1,0:T(8,128)(2,1)S(1)}, u32[]{:S(2)}, u32[]{:S(2)}) collective-permute-start(bf16[2,128,1024]{2,1,0:T(8,128)(2,1)S(1)} %slice_bitcast_fusion), channel_id=1, source_target_pairs={{0,192},{32,224},{64,0},{96,32},{128,64},{160,96},{192,128},{224,1... | collective-permute-start | bytes 1572872 | tf_op jit(solution)/shard_map/ppermute | solution.py:222
  105.9 1.8 fusion.9
  107.8 1.9 fusion.8
  110.1 0.9 fusion.7
  110.9 3.6 %collective-permute-done.7 = bf16[2,128,1024]{2,1,0:T(8,128)(2,1)S(1)} collective-permute-done((bf16[2,128,1024]{2,1,0:T(8,128)(2,1)S(1)}, bf16[2,128,1024]{2,1,0:T(8,128)(2,1)S(1)}, u32[]{:S(2)}, u32[]{:S(2)}) %collective-permute-start.7) | collective-permute-done | bytes 524320 | tf_op jit(solution)/shard_map/ppermute | solution.py:222
  114.5 0.8 fusion.6
  115.4 1.8 fusion.5
  117.2 1.9 fusion.4
  119.2 0.8 copy-done.12
  120.0 1.9 collective-permute-start.9
  121.9 1.4 collective-permute-done.10.rest_2_
  123.3 0.8 copy-done.14
  124.1 8.9 %collective-permute-done.11.rest_3_ = bf16[256,1024]{1,0:T(8,128)(2,1)S(1)} collective-permute-done((bf16[256,1024]{1,0:T(8,128)(2,1)S(1)}, bf16[256,1024]{1,0:T(8,128)(2,1)S(1)}, u32[]{:S(2)}, u32[]{:S(2)}) %collective-permute-start.11) | collective-permute-done | bytes 524320 | tf_op jit(solution)/shard_map/ppermute | solution.py:222
  133.0 0.8 copy-done.16
  133.9 1.9 collective-permute-start.12
  139.9 3.8 %exp_scores.2 = (f32[128,2048]{1,0:T(8,128)S(1)}, f32[128,1]{1,0:T(8,128)S(1)}) custom-call(bf16[128,1024]{1,0:T(8,128)(2,1)S(1)} %copy-done.2, bf16[1024,1024]{1,0:T(8,128)(2,1)} %get-tuple-element.32.own_ref.own, bf16[1024,1024]{1,0:T(8,128)(2,1)} %collective-permute-done.9.other_ref.other), custom_call_target="tpu_custom_call" | custom-call | flops 536870912 | bytes 5505024 | tf_op jit(solution)/shard_map/exp_scores/pallas_call | solution.py:105
  143.7 0.9 copy-done.4
  145.3 0.8 copy-done.25
  146.1 1.1 totals.1
  149.1 5.1 %all-to-all-start.2 = ((f32[16,2,128]{2,1,0:T(2,128)}), f32[16,2,128]{2,1,0:T(2,128)S(1)}, u32[]{:S(2)}, u32[]{:S(2)}) async-start(f32[16,2,128]{2,1,0:T(2,128)} %copy-done.27), calls=%async_computation.2 | async-start | bytes 32768 | tf_op jit(solution)/shard_map/all_to_all | solution.py:215
  156.3 1.0 select_reduce_fusion.2
  157.3 0.9 copy-done.9
  158.2 4.5 %exp_scores.3 = (f32[128,2048]{1,0:T(8,128)S(1)}, f32[128,1]{1,0:T(8,128)}) custom-call(bf16[128,1024]{1,0:T(8,128)(2,1)S(1)} %copy-done.9, bf16[1024,1024]{1,0:T(8,128)(2,1)} %get-tuple-element.34.own_ref.own, bf16[1024,1024]{1,0:T(8,128)(2,1)} %collective-permute-done.12.other_ref.other), custom_call_target="tpu_custom_call" | custom-call | flops 536870912 | bytes 5505024 | tf_op jit(solution)/shard_map/exp_scores/pallas_call | solution.py:105
  162.7 1.0 copy-done.10
  165.6 12.2 %all-to-all-start.3 = ((f32[32,2,32]{2,1,0:T(2,128)}), f32[32,2,32]{2,1,0:T(2,128)}, u32[]{:S(2)}, u32[]{:S(2)}) async-start(f32[32,2,32]{2,1,0:T(2,128)} %copy.14), calls=%async_computation.3 | async-start | bytes 65536 | tf_op jit(solution)/shard_map/all_to_all | solution.py:215
  177.9 1.2 copy-done.5
  179.1 0.8 copy-done.21
  179.9 0.8 copy-done.23
  180.8 4.4 %gradients.2 = bf16[128,1024]{1,0:T(8,128)(2,1)} custom-call(f32[128,2048]{1,0:T(8,128)S(1)} %copy-done.5, f32[128,1]{1,0:T(8,128)S(1)} %copy-done.23, s32[128,1]{1,0:T(8,128)S(1)} %copy.13.mark_ref, s32[1,2048]{1,0:T(1,128)S(1)} %bitcast.203, bf16[1024,1024]{1,0:T(8,128)(2,1)} %get-tuple-element.32.own_ref.own, ...), custom_call_target="tpu_custom_call" | custom-call | flops 805306368 | bytes 8126464 | tf_op jit(solution)/shard_map/gradients/pallas_call | solution.py:195
  185.2 4.7 %all-to-all-done.3 = f32[32,2,32]{2,1,0:T(2,128)} async-done(((f32[32,2,32]{2,1,0:T(2,128)}), f32[32,2,32]{2,1,0:T(2,128)}, u32[]{:S(2)}, u32[]{:S(2)}) %all-to-all-start.3) | async-done | bytes 8224 | tf_op jit(solution)/shard_map/all_to_all | solution.py:215
  189.9 0.8 copy.15
  191.7 1.2 copy-done.11
  192.9 1.0 copy-done.13
  193.9 1.0 copy-done.15
  195.0 1.0 copy-done.17
  196.0 0.8 copy-done.20
  197.6 4.4 %gradients.3 = bf16[128,1024]{1,0:T(8,128)(2,1)} custom-call(f32[128,2048]{1,0:T(8,128)S(1)} %copy-done.11, f32[1,2048]{1,0:T(1,128)S(1)} %copy-done.26, s32[128,1]{1,0:T(8,128)S(1)} %iota_add_fusion.mark_ref, s32[1,2048]{1,0:T(1,128)S(1)} %get-tuple-element.72.marks_ref, bf16[1024,1024]{1,0:T(8,128)(2,1)} %get-tuple-element.34.own_ref.own, ...), custom_call_target="tpu_custom_call" | custom-call | flops 805306368 | bytes 8126464 | tf_op jit(solution)/shard_map/gradients/pallas_call | solution.py:195
  (110 shorter events, 14.8 us)
Async XLA Ops:
  7.2 51.6 %all-gather.2.cloned.1.call-start = ((), (), s32[]{:S(2)}) async-start(), calls=%async_computation.4 | async-start | bytes 2359296 | tf_op jit(solution)/shard_map/all_gather | solution.py:283
  9.4 62.2 %collective-permute-start.2 = (bf16[128,1024]{1,0:T(8,128)(2,1)}, bf16[128,1024]{1,0:T(8,128)(2,1)S(1)}, u32[]{:S(2)}, u32[]{:S(2)}) collective-permute-start(bf16[128,1024]{1,0:T(8,128)(2,1)} %get-tuple-element.28.x_ref), channel_id=1, source_target_pairs={{0,8},{1,9},{2,10},{3,11},{4,12},{5,13},{6,14},{7,15},{8,16},{9,17... | collective-permute-start | bytes 786440 | tf_op jit(solution)/shard_map/ppermute | solution.py:222
  15.5 56.1 %collective-permute-start.1 = (bf16[128,1024]{1,0:T(8,128)(2,1)}, bf16[128,1024]{1,0:T(8,128)(2,1)S(1)}, u32[]{:S(2)}, u32[]{:S(2)}) collective-permute-start(bf16[128,1024]{1,0:T(8,128)(2,1)} %get-tuple-element.28.x_ref), channel_id=1, source_target_pairs={{0,16},{1,17},{2,18},{3,19},{4,20},{5,21},{6,22},{7,23},{8,24},{9,... | collective-permute-start | bytes 786440 | tf_op jit(solution)/shard_map/ppermute | solution.py:222
  24.6 47.0 %collective-permute-start = (bf16[128,1024]{1,0:T(8,128)(2,1)}, bf16[128,1024]{1,0:T(8,128)(2,1)S(1)}, u32[]{:S(2)}, u32[]{:S(2)}) collective-permute-start(bf16[128,1024]{1,0:T(8,128)(2,1)} %get-tuple-element.28.x_ref), channel_id=1, source_target_pairs={{0,24},{1,25},{2,26},{3,27},{4,28},{5,29},{6,30},{7,31},{8,0},{9,1... | collective-permute-start | bytes 786440 | tf_op jit(solution)/shard_map/ppermute | solution.py:222
  29.6 15.0 %all-to-all-start = ((s32[8,1,512]{2,1,0:T(1,128)}), s32[8,1,512]{2,1,0:T(1,128)S(1)}, u32[]{:S(2)}, u32[]{:S(2)}) async-start(s32[8,1,512]{2,1,0:T(1,128)} %broadcast_in_dim.129), calls=%async_computation | async-start | bytes 32768 | tf_op jit(solution)/shard_map/all_to_all | solution.py:215
  36.7 27.2 %collective-permute-start.3 = (bf16[2,128,1024]{2,1,0:T(8,128)(2,1)}, bf16[2,128,1024]{2,1,0:T(8,128)(2,1)S(1)}, u32[]{:S(2)}, u32[]{:S(2)}) collective-permute-start(bf16[2,128,1024]{2,1,0:T(8,128)(2,1)} %get-tuple-element.29), channel_id=1, source_target_pairs={{0,256},{32,288},{64,320},{96,352},{128,384},{160,416},{192,448},{... | collective-permute-start | bytes 1572872 | tf_op jit(solution)/shard_map/ppermute | solution.py:222
  58.7 1.6 copy-start.3
  60.3 3.5 %copy-start.31 = (bf16[2,128,1024]{2,1,0:T(8,128)(2,1)S(1)}, bf16[2,128,1024]{2,1,0:T(8,128)(2,1)}, u32[]{:S(2)}) copy-start(bf16[2,128,1024]{2,1,0:T(8,128)(2,1)} %get-tuple-element.29) | copy-start | bytes 1572868
  62.5 1.4 copy-start
  63.9 7.8 %copy-start.8 = (bf16[128,1024]{1,0:T(8,128)(2,1)S(1)}, bf16[128,1024]{1,0:T(8,128)(2,1)}, u32[]{:S(2)}) copy-start(bf16[128,1024]{1,0:T(8,128)(2,1)} %get-tuple-element.28.x_ref) | copy-start | bytes 786436
  63.9 8.0 %copy-start.29 = (bf16[2,128,1024]{2,1,0:T(8,128)(2,1)}, bf16[2,128,1024]{2,1,0:T(8,128)(2,1)S(1)}, u32[]{:S(2)}) copy-start(bf16[2,128,1024]{2,1,0:T(8,128)(2,1)S(1)} %collective-permute-done.3) | copy-start | bytes 1572868
  64.9 33.0 %collective-permute-start.4 = (bf16[2,2,128,1024]{3,2,1,0:T(8,128)(2,1)}, bf16[2,2,128,1024]{3,2,1,0:T(8,128)(2,1)}, u32[]{:S(2)}, u32[]{:S(2)}) collective-permute-start(bf16[2,2,128,1024]{3,2,1,0:T(8,128)(2,1)} %pad_maximum_fusion.1), channel_id=1, source_target_pairs={{0,64},{32,96},{64,128},{96,160},{128,192},{160,224},{192,0},{224,... | collective-permute-start | bytes 3145736 | tf_op jit(solution)/shard_map/ppermute | solution.py:222
  69.1 33.2 %collective-permute-start.6 = (bf16[2,2,128,1024]{3,2,1,0:T(8,128)(2,1)}, bf16[2,2,128,1024]{3,2,1,0:T(8,128)(2,1)}, u32[]{:S(2)}, u32[]{:S(2)}) collective-permute-start(bf16[2,2,128,1024]{3,2,1,0:T(8,128)(2,1)} %pad_maximum_fusion.1), channel_id=1, source_target_pairs={{0,192},{32,224},{64,0},{96,32},{128,64},{160,96},{192,128},{224,1... | collective-permute-start | bytes 3145736 | tf_op jit(solution)/shard_map/ppermute | solution.py:222
  73.3 1.3 copy-start.1
  74.6 70.7 %all-to-all-start.1 = ((bf16[8,128,1024]{2,1,0:T(8,128)(2,1)}), bf16[8,128,1024]{2,1,0:T(8,128)(2,1)S(1)}, u32[]{:S(2)}, u32[]{:S(2)}) async-start(bf16[8,128,1024]{2,1,0:T(8,128)(2,1)} %bitcast.200), calls=%async_computation.1 | async-start | bytes 4194304 | tf_op jit(solution)/shard_map/all_to_all | solution.py:215
  79.4 17.7 %copy-start.30 = (bf16[2,128,1024]{2,1,0:T(8,128)(2,1)S(1)}, bf16[2,128,1024]{2,1,0:T(8,128)(2,1)}, u32[]{:S(2)}) copy-start(bf16[2,128,1024]{2,1,0:T(8,128)(2,1)} %copy-done.29) | copy-start | bytes 1572868
  81.2 37.9 %collective-permute-start.8 = (bf16[256,1024]{1,0:T(8,128)(2,1)S(1)}, bf16[256,1024]{1,0:T(8,128)(2,1)S(1)}, u32[]{:S(2)}, u32[]{:S(2)}) collective-permute-start(bf16[256,1024]{1,0:T(8,128)(2,1)S(1)} %get-tuple-element.55), channel_id=1, source_target_pairs={{0,8},{1,9},{2,10},{3,11},{4,12},{5,13},{6,14},{7,15},{8,16},{9,17... | collective-permute-start | bytes 1572872 | tf_op jit(solution)/shard_map/ppermute | solution.py:222
  85.6 37.7 %collective-permute-start.10 = (bf16[256,1024]{1,0:T(8,128)(2,1)S(1)}, bf16[256,1024]{1,0:T(8,128)(2,1)S(1)}, u32[]{:S(2)}, u32[]{:S(2)}) collective-permute-start(bf16[256,1024]{1,0:T(8,128)(2,1)S(1)} %get-tuple-element.54), channel_id=1, source_target_pairs={{0,16},{1,17},{2,18},{3,19},{4,20},{5,21},{6,22},{7,23},{8,24},{9,... | collective-permute-start | bytes 1572872 | tf_op jit(solution)/shard_map/ppermute | solution.py:222
  91.5 41.6 %collective-permute-start.11 = (bf16[256,1024]{1,0:T(8,128)(2,1)S(1)}, bf16[256,1024]{1,0:T(8,128)(2,1)S(1)}, u32[]{:S(2)}, u32[]{:S(2)}) collective-permute-start(bf16[256,1024]{1,0:T(8,128)(2,1)S(1)} %get-tuple-element.53), channel_id=1, source_target_pairs={{0,24},{1,25},{2,26},{3,27},{4,28},{5,29},{6,30},{7,31},{8,0},{9,1... | collective-permute-start | bytes 1572872 | tf_op jit(solution)/shard_map/ppermute | solution.py:222
  99.0 11.1 %collective-permute-start.5 = (bf16[2,128,1024]{2,1,0:T(8,128)(2,1)S(1)}, bf16[2,128,1024]{2,1,0:T(8,128)(2,1)S(1)}, u32[]{:S(2)}, u32[]{:S(2)}) collective-permute-start(bf16[2,128,1024]{2,1,0:T(8,128)(2,1)S(1)} %slice_bitcast_fusion.1), channel_id=1, source_target_pairs={{0,64},{32,96},{64,128},{96,160},{128,192},{160,224},{192,0},{224,... | collective-permute-start | bytes 1572872 | tf_op jit(solution)/shard_map/ppermute | solution.py:222
  103.5 11.1 %collective-permute-start.7 = (bf16[2,128,1024]{2,1,0:T(8,128)(2,1)S(1)}, bf16[2,128,1024]{2,1,0:T(8,128)(2,1)S(1)}, u32[]{:S(2)}, u32[]{:S(2)}) collective-permute-start(bf16[2,128,1024]{2,1,0:T(8,128)(2,1)S(1)} %slice_bitcast_fusion), channel_id=1, source_target_pairs={{0,192},{32,224},{64,0},{96,32},{128,64},{160,96},{192,128},{224,1... | collective-permute-start | bytes 1572872 | tf_op jit(solution)/shard_map/ppermute | solution.py:222
  110.1 25.7 %copy-start.32 = (s32[128,4]{0,1:T(4,128)S(1)}, s32[128,4]{0,1:T(4,128)}, u32[]{:S(2)}) copy-start(s32[128,4]{0,1:T(4,128)} %param.8) | copy-start | bytes 6148
  110.1 25.7 %copy-start.33 = (s32[128]{0:T(128)S(1)}, s32[128]{0:T(128)}, u32[]{:S(2)}) copy-start(s32[128]{0:T(128)} %param.9) | copy-start | bytes 1540
  110.9 26.3 %copy-start.28 = (s32[128]{0:T(128)S(1)}, s32[128]{0:T(128)}, u32[]{:S(2)}) copy-start(s32[128]{0:T(128)} %param.7) | copy-start | bytes 1540
  114.5 25.3 %copy-start.2 = (bf16[128,1024]{1,0:T(8,128)(2,1)S(1)}, bf16[128,1024]{1,0:T(8,128)(2,1)}, u32[]{:S(2)}) copy-start(bf16[128,1024]{1,0:T(8,128)(2,1)} %get-tuple-element.27.x_ref.q_ref) | copy-start | bytes 786436
  119.2 0.8 copy-start.12
  120.0 19.9 %collective-permute-start.9 = (bf16[1024,1024]{1,0:T(8,128)(2,1)}, bf16[1024,1024]{1,0:T(8,128)(2,1)}, u32[]{:S(2)}, u32[]{:S(2)}) collective-permute-start(bf16[1024,1024]{1,0:T(8,128)(2,1)} %get-tuple-element.32.own_ref.own), channel_id=1, source_target_pairs={{0,32},{32,0},{64,96},{96,64},{128,160},{160,128},{192,224},{224,1... | collective-permute-start | bytes 6291464 | tf_op jit(solution)/shard_map/ppermute | solution.py:222
  123.3 0.8 copy-start.14
  133.0 0.8 copy-start.16
  133.9 11.4 %collective-permute-start.12 = (bf16[1024,1024]{1,0:T(8,128)(2,1)}, bf16[1024,1024]{1,0:T(8,128)(2,1)}, u32[]{:S(2)}, u32[]{:S(2)}) collective-permute-start(bf16[1024,1024]{1,0:T(8,128)(2,1)} %get-tuple-element.34.own_ref.own), channel_id=1, source_target_pairs={{0,32},{32,0},{64,96},{96,64},{128,160},{160,128},{192,224},{224,1... | collective-permute-start | bytes 6291464 | tf_op jit(solution)/shard_map/ppermute | solution.py:222
  143.7 1.0 copy-start.4
  144.7 0.6 copy-start.24
  145.3 0.8 copy-start.25
  147.2 0.7 copy-start.18
  147.9 0.6 copy-start.22
  148.5 0.6 copy-start.27
  149.1 14.6 %all-to-all-start.2 = ((f32[16,2,128]{2,1,0:T(2,128)}), f32[16,2,128]{2,1,0:T(2,128)S(1)}, u32[]{:S(2)}, u32[]{:S(2)}) async-start(f32[16,2,128]{2,1,0:T(2,128)} %copy-done.27), calls=%async_computation.2 | async-start | bytes 32768 | tf_op jit(solution)/shard_map/all_to_all | solution.py:215
  157.2 1.0 copy-start.9
  158.2 19.7 %copy-start.6 = (bf16[128,1024]{1,0:T(8,128)(2,1)S(1)}, bf16[128,1024]{1,0:T(8,128)(2,1)}, u32[]{:S(2)}) copy-start(bf16[128,1024]{1,0:T(8,128)(2,1)} %x_ref.2) | copy-start | bytes 786436
  158.2 19.7 %copy-start.19 = (bf16[128,1024]{1,0:T(8,128)(2,1)S(1)}, bf16[128,1024]{1,0:T(8,128)(2,1)}, u32[]{:S(2)}) copy-start(bf16[128,1024]{1,0:T(8,128)(2,1)} %copy-done.18) | copy-start | bytes 786436
  162.7 1.0 copy-start.10
  165.6 24.3 %all-to-all-start.3 = ((f32[32,2,32]{2,1,0:T(2,128)}), f32[32,2,32]{2,1,0:T(2,128)}, u32[]{:S(2)}, u32[]{:S(2)}) async-start(f32[32,2,32]{2,1,0:T(2,128)} %copy.14), calls=%async_computation.3 | async-start | bytes 65536 | tf_op jit(solution)/shard_map/all_to_all | solution.py:215
  177.9 1.2 copy-start.5
  179.1 0.8 copy-start.21
  179.9 0.8 copy-start.23
  180.8 10.9 %copy-start.7 = (bf16[128,1024]{1,0:T(8,128)(2,1)S(1)}, bf16[128,1024]{1,0:T(8,128)(2,1)}, u32[]{:S(2)}) copy-start(bf16[128,1024]{1,0:T(8,128)(2,1)} %x_ref.3) | copy-start | bytes 786436
  191.7 1.2 copy-start.11
  192.9 1.0 copy-start.13
  193.9 1.0 copy-start.15
  195.0 1.0 copy-start.17
  196.0 0.8 copy-start.20
  196.9 0.7 copy-start.26
Sparse Core Ops, SparseCore 0:
  10.7 48.0 all-gather.1
where the time goes:
time: 210 us; the launch traced here: 209 us
  starting transfers between devices  82.9 us (39%)
  local copies, waits for them, and re-layouts  43.1 us (21%)
  waiting for transfers between devices  34 us (16%)
  Pallas kernels  23.9 us (11%)
  between operations  15.4 us (7%)
  other arithmetic  9.26 us (4%)
    ppermute x13, starting transfers between devices, shifted(): return lax.ppermute(value, axis, [(i, move(i)) for i in range(devices)])  53.6 us
    unnamed x75, local copies, waits for them, and re-layouts  31.7 us
    all_to_all x4, starting transfers between devices, exchange(): lax.all_to_all(value, axis, split_axis=0, concat_axis=0, tiled=True, axis...  29.3 us
    ppermute x13, waiting for transfers between devices, shifted(): return lax.ppermute(value, axis, [(i, move(i)) for i in range(devices)])  14.4 us
    all_gather x1, waiting for transfers between devices, local(): lax.all_gather(q_half, 'dp', axis=0, tiled=True, axis_index_groups=lines)  13.2 us
    pallas_call x2, Pallas kernels, grads_of(): pl.pallas_call(grad_kernel, in_specs=[whole] * len(operands) + [pl.BlockS...  8.73 us
    pallas_call x2, Pallas kernels, exp_scores_of(): pl.pallas_call(exp_kernel, out_shape=(jax.ShapeDtypeStruct((rows, 2 * own...  8.3 us
    all_to_all x4, waiting for transfers between devices, exchange(): lax.all_to_all(value, axis, split_axis=0, concat_axis=0, tiled=True, axis...  6.46 us
  transfers between devices with their start and end apart: 18, of which 7 were waited for; matrix products, arithmetic and copies ran while one was open for 13% of the time, Pallas kernels for 8%

commit v1 on v0

--- a/solution.py
+++ b/solution.py
@@ -7,6 +7,7 @@
 
 EPS = 1e-06
 TAU = 0.02
+ROOMY = pltpu.CompilerParams(vmem_limit_bytes=56 * 1024 * 1024)
 
 
 def unit_rows(x):
@@ -62,7 +63,7 @@
         ],
         out_specs=pl.BlockSpec((parts, 1, ranks, width), lambda g: (0, g, 0, 0)),
         out_shape=jax.ShapeDtypeStruct((parts, groups, ranks, width), jnp.bfloat16),
-        compiler_params=room(4),
+        compiler_params=ROOMY,
         cost_estimate=pl.CostEstimate(
             flops=2 * groups * rows * parts * ranks * width,
             bytes_accessed=2 * groups * (rows + parts * ranks) * width,
@@ -74,10 +75,6 @@
 
 
 TILE = 256
-
-
-def room(mib):
-    return pltpu.CompilerParams(vmem_limit_bytes=mib * 1024 * 1024)
 
 
 def cost(rows, width, columns, exps=0):
@@ -108,7 +105,7 @@
             jax.ShapeDtypeStruct((rows, 2 * own.shape[0]), jnp.float32),
             jax.ShapeDtypeStruct((rows, 1), jnp.float32),
         ),
-        compiler_params=room(8),
+        compiler_params=ROOMY,
         cost_estimate=cost(rows, x.shape[1], 2 * own.shape[0], 2 * rows * own.shape[0]),
         name="exp_scores",
     )(x, own, other)
@@ -148,7 +145,7 @@
             jax.ShapeDtypeStruct((1, slots), jnp.float32),
             jax.ShapeDtypeStruct((length, 2, rows), jnp.float32),
         ),
-        compiler_params=room(8),
+        compiler_params=ROOMY,
         cost_estimate=cost(rows, q_half.shape[1], slots, rows * slots),
         name="totals",
     )(q_half, hard_rows, mask, sums, positive.reshape(1, rows))
@@ -201,7 +198,7 @@
             pltpu.VMEM((weights.shape[1], x.shape[1]), jnp.bfloat16),
             pltpu.SemaphoreType.DMA((len(hard),)),
         ],
-        compiler_params=room(12),
+        compiler_params=ROOMY,
         cost_estimate=cost(*x.shape, exps.shape[1] + weights.shape[1]),
         name="gradients",
     )(*operands, *hard)
@@ -305,9 +302,9 @@
     asked_by = table % (2 * rows) - 1
 
     sent_p = pick_rows(asked_row, p_line)
+    asked_by, sent_p = lax.optimization_barrier((asked_by, sent_p))
+    sent_q = pick_rows(jnp.swapaxes(asked_by, 0, 1), q_line.reshape(ny, rows, width))
     got_p = exchange(sent_p, "dp", lines).reshape(slots, width)
-
-    sent_q = pick_rows(jnp.swapaxes(asked_by, 0, 1), q_line.reshape(ny, rows, width))
     (p_own, q_own), sent_q = gather_chips(both, sent_q)
     got_q = [sent_q[0]]
     got_q += [shifted(sent_q[t], "dp", lambda i, t=t: along_z(i, t)) for t in range(1, nz)]

time: 210 us -> 202 us (0.962)
  local copies, waits for them, and re-layouts: 43.1 us -> 19.1 us
  Pallas kernels: 23.9 us -> 37.4 us
    unnamed x75 -> x21, local copies, waits for them, and re-layouts: 31.7 us -> 9.34 us
    all_gather x1, waiting for transfers between devices: 13.2 us -> 3 us  [local(): lax.all_gather(q_half, 'dp', axis=0, tiled=True, axis_index_groups=lines)]
    pallas_call x2, Pallas kernels: 3.59 us -> 10.9 us  [pick_rows(): pl.pallas_call(pick_kernel, grid=(groups,), in_specs=[pl.BlockSpec((1, 1,...]
    ppermute x13, waiting for transfers between devices: 14.4 us -> 21.6 us  [shifted(): return lax.ppermute(value, axis, [(i, move(i)) for i in range(devices)])]
    all_to_all x4, waiting for transfers between devices: 6.46 us -> 10.8 us  [exchange(): lax.all_to_all(value, axis, split_axis=0, concat_axis=0, tiled=True, axis...]
    pallas_call x1, Pallas kernels: 1.08 us -> 3.53 us  [totals_of(): pl.pallas_call(total_kernel, out_shape=(jax.ShapeDtypeStruct((rows, 1), j...]
    pallas_call x2, Pallas kernels: 8.73 us -> 11.1 us  [grads_of(): pl.pallas_call(grad_kernel, in_specs=[whole] * len(operands) + [pl.BlockS...]
  transfers between devices with their start and end apart: 18 -> 18, of which waited for: 7 -> 8; matrix products, arithmetic and copies ran while one was open for 13% -> 12% of each run, Pallas kernels for 8% -> 13%
where the time goes in v1:
time: 202 us; the launch traced here: 201 us
  starting transfers between devices  82.8 us (41%)
  Pallas kernels  37.4 us (19%)
  waiting for transfers between devices  35.4 us (18%)
  local copies, waits for them, and re-layouts  19.1 us (9%)
  between operations  14.9 us (7%)
  other arithmetic  10.9 us (5%)
    ppermute x13, starting transfers between devices, shifted(): return lax.ppermute(value, axis, [(i, move(i)) for i in range(devices)])  53.5 us
    all_to_all x4, starting transfers between devices, exchange(): lax.all_to_all(value, axis, split_axis=0, concat_axis=0, tiled=True, axis...  29.3 us
    ppermute x13, waiting for transfers between devices, shifted(): return lax.ppermute(value, axis, [(i, move(i)) for i in range(devices)])  21.6 us
    pallas_call x2, Pallas kernels, grads_of(): pl.pallas_call(grad_kernel, in_specs=[whole] * len(operands) + [pl.BlockS...  11.1 us
    pallas_call x2, Pallas kernels, pick_rows(): pl.pallas_call(pick_kernel, grid=(groups,), in_specs=[pl.BlockSpec((1, 1,...  10.9 us
    all_to_all x4, waiting for transfers between devices, exchange(): lax.all_to_all(value, axis, split_axis=0, concat_axis=0, tiled=True, axis...  10.8 us
    pallas_call x2, Pallas kernels, exp_scores_of(): pl.pallas_call(exp_kernel, out_shape=(jax.ShapeDtypeStruct((rows, 2 * own...  9.64 us
    unnamed x21, local copies, waits for them, and re-layouts  9.34 us
  transfers between devices with their start and end apart: 18, of which 8 were waited for; matrix products, arithmetic and copies ran while one was open for 12% of the time, Pallas kernels for 13%

profile of v1, /device:TPU:2, one launch (start us, length us, event | category | flops | bytes accessed | tf_op | source)
XLA Modules:
  0.0 200.8 jit_solution(71398899068594640)
XLA Ops:
  7.2 2.2 %unit_halves.1 = (bf16[128,1024]{1,0:T(8,128)(2,1)}, bf16[128,1024]{1,0:T(8,128)(2,1)}, bf16[2,128,1024]{2,1,0:T(8,128)(2,1)}, f32[128,1]{1,0:T(8,128)}, f32[128,1]{1,0:T(8,128)}) custom-call(bf16[128,1024]{1,0:T(8,128)(2,1)} %x_ref.2, bf16[128,1024]{1,0:T(8,128)(2,1)} %x_ref.3), custom_call_target="tpu_custom_call" | custom-call | flops 1048576 | bytes 1572864 | tf_op jit(solution)/shard_map/unit_halves/pallas_call | solution.py:31
  9.4 6.1 %collective-permute-start.2 = (bf16[128,1024]{1,0:T(8,128)(2,1)}, bf16[128,1024]{1,0:T(8,128)(2,1)S(1)}, u32[]{:S(2)}, u32[]{:S(2)}) collective-permute-start(bf16[128,1024]{1,0:T(8,128)(2,1)} %get-tuple-element.30.x_ref), channel_id=1, source_target_pairs={{0,8},{1,9},{2,10},{3,11},{4,12},{5,13},{6,14},{7,15},{8,16},{9,17... | collective-permute-start | bytes 786440 | tf_op jit(solution)/shard_map/ppermute | solution.py:219
  15.5 9.1 %collective-permute-start.1 = (bf16[128,1024]{1,0:T(8,128)(2,1)}, bf16[128,1024]{1,0:T(8,128)(2,1)S(1)}, u32[]{:S(2)}, u32[]{:S(2)}) collective-permute-start(bf16[128,1024]{1,0:T(8,128)(2,1)} %get-tuple-element.30.x_ref), channel_id=1, source_target_pairs={{0,16},{1,17},{2,18},{3,19},{4,20},{5,21},{6,22},{7,23},{8,24},{9,... | collective-permute-start | bytes 786440 | tf_op jit(solution)/shard_map/ppermute | solution.py:219
  24.7 3.7 %collective-permute-start = (bf16[128,1024]{1,0:T(8,128)(2,1)}, bf16[128,1024]{1,0:T(8,128)(2,1)S(1)}, u32[]{:S(2)}, u32[]{:S(2)}) collective-permute-start(bf16[128,1024]{1,0:T(8,128)(2,1)} %get-tuple-element.30.x_ref), channel_id=1, source_target_pairs={{0,24},{1,25},{2,26},{3,27},{4,28},{5,29},{6,30},{7,31},{8,0},{9,1... | collective-permute-start | bytes 786440 | tf_op jit(solution)/shard_map/ppermute | solution.py:219
  28.3 1.3 broadcast_in_dim.129
  29.6 7.1 %all-to-all-start = ((s32[8,1,512]{2,1,0:T(1,128)}), s32[8,1,512]{2,1,0:T(1,128)S(1)}, u32[]{:S(2)}, u32[]{:S(2)}) async-start(s32[8,1,512]{2,1,0:T(1,128)} %broadcast_in_dim.129), calls=%async_computation | async-start | bytes 32768 | tf_op jit(solution)/shard_map/all_to_all | solution.py:212
  36.7 3.4 %collective-permute-start.3 = (bf16[2,128,1024]{2,1,0:T(8,128)(2,1)}, bf16[2,128,1024]{2,1,0:T(8,128)(2,1)S(1)}, u32[]{:S(2)}, u32[]{:S(2)}) collective-permute-start(bf16[2,128,1024]{2,1,0:T(8,128)(2,1)} %get-tuple-element.32), channel_id=1, source_target_pairs={{0,256},{32,288},{64,320},{96,352},{128,384},{160,416},{192,448},{... | collective-permute-start | bytes 1572872 | tf_op jit(solution)/shard_map/ppermute | solution.py:219
  40.3 4.3 %all-to-all-done = s32[8,1,512]{2,1,0:T(1,128)S(1)} async-done(((s32[8,1,512]{2,1,0:T(1,128)}), s32[8,1,512]{2,1,0:T(1,128)S(1)}, u32[]{:S(2)}, u32[]{:S(2)}) %all-to-all-start) | async-done | bytes 16416 | tf_op jit(solution)/shard_map/all_to_all | solution.py:212
  44.9 0.6 select_reduce_fusion.1
  45.6 0.6 fusion.27.index_ref
  46.2 2.5 %collective-permute-done = bf16[128,1024]{1,0:T(8,128)(2,1)S(1)} collective-permute-done((bf16[128,1024]{1,0:T(8,128)(2,1)}, bf16[128,1024]{1,0:T(8,128)(2,1)S(1)}, u32[]{:S(2)}, u32[]{:S(2)}) %collective-permute-start) | collective-permute-done | bytes 262176 | tf_op jit(solution)/shard_map/ppermute | solution.py:219
  48.7 2.1 %pad_maximum_fusion.pool_ref = bf16[4,128,1024]{2,1,0:T(8,128)(2,1)} fusion(bf16[1,128,1024]{2,1,0:T(8,128)(2,1)S(1)} %bitcast.202, bf16[1,128,1024]{2,1,0:T(8,128)(2,1)S(1)} %bitcast.203, bf16[1,128,1024]{2,1,0:T(8,128)(2,1)S(1)} %bitcast.204, bf16[1,128,1024]{2,1,0:T(8,128)(2,1)} %bitcast.201), kind=kLoop, calls=%fused_computation.9 | loop fusion | flops 1572864 | bytes 2097152 | tf_op jit(solution)/shard_map/stack | solution.py:287
  50.8 4.3 %pick_rows.2 = bf16[8,4,32,1024]{3,2,1,0:T(8,128)(2,1)} custom-call(s32[4,1,256]{2,1,0:T(1,128)} %fusion.27.index_ref, bf16[4,128,1024]{2,1,0:T(8,128)(2,1)} %pad_maximum_fusion.pool_ref), custom_call_target="tpu_custom_call" | custom-call | flops 268435456 | bytes 3145728 | tf_op jit(solution)/shard_map/pick_rows/pallas_call | solution.py:57
  55.1 0.7 reshape.1216.index_ref
  55.7 3.0 %all-gather.2.cloned.1.call-done = bf16[1024,1024]{1,0:T(8,128)(2,1)} async-done(((bf16[128,1024]{1,0:T(8,128)(2,1)}), bf16[1024,1024]{1,0:T(8,128)(2,1)}) %all-gather.2.cloned.1.call-update) | async-done | bytes 2097168 | tf_op jit(solution)/shard_map/all_gather | solution.py:280
  58.7 6.6 %pick_rows.3 = bf16[4,8,32,1024]{3,2,1,0:T(8,128)(2,1)} custom-call(s32[8,1,128]{2,1,0:T(1,128)} %reshape.1216.index_ref, bf16[8,128,1024]{2,1,0:T(8,128)(2,1)} %bitcast.198), custom_call_target="tpu_custom_call" | custom-call | flops 268435456 | bytes 4194304 | tf_op jit(solution)/shard_map/pick_rows/pallas_call | solution.py:57
  65.4 1.2 pad_maximum_fusion.1
  66.6 3.4 %collective-permute-start.4 = (bf16[2,2,128,1024]{3,2,1,0:T(8,128)(2,1)}, bf16[2,2,128,1024]{3,2,1,0:T(8,128)(2,1)}, u32[]{:S(2)}, u32[]{:S(2)}) collective-permute-start(bf16[2,2,128,1024]{3,2,1,0:T(8,128)(2,1)} %pad_maximum_fusion.1), channel_id=1, source_target_pairs={{0,64},{32,96},{64,128},{96,160},{128,192},{160,224},{192,0},{224,... | collective-permute-start | bytes 3145736 | tf_op jit(solution)/shard_map/ppermute | solution.py:219
  70.0 0.2 convert_reduce_fusion
  70.2 2.5 %collective-permute-start.6 = (bf16[2,2,128,1024]{3,2,1,0:T(8,128)(2,1)}, bf16[2,2,128,1024]{3,2,1,0:T(8,128)(2,1)S(1)}, u32[]{:S(2)}, u32[]{:S(2)}) collective-permute-start(bf16[2,2,128,1024]{3,2,1,0:T(8,128)(2,1)} %pad_maximum_fusion.1), channel_id=1, source_target_pairs={{0,192},{32,224},{64,0},{96,32},{128,64},{160,96},{192,128},{224,1... | collective-permute-start | bytes 3145736 | tf_op jit(solution)/shard_map/ppermute | solution.py:219
  73.2 0.9 bitcast_dynamic-update-slice_fusion.1
  74.1 4.9 %all-to-all-start.1 = ((bf16[8,128,1024]{2,1,0:T(8,128)(2,1)}), bf16[8,128,1024]{2,1,0:T(8,128)(2,1)S(1)}, u32[]{:S(2)}, u32[]{:S(2)}) async-start(bf16[8,128,1024]{2,1,0:T(8,128)(2,1)} %bitcast.197), calls=%async_computation.1 | async-start | bytes 4194304 | tf_op jit(solution)/shard_map/all_to_all | solution.py:212
  78.9 2.6 %slice_bitcast_fusion.2 = (bf16[256,1024]{1,0:T(8,128)(2,1)}, bf16[256,1024]{1,0:T(8,128)(2,1)S(1)}, bf16[256,1024]{1,0:T(8,128)(2,1)S(1)}, bf16[256,1024]{1,0:T(8,128)(2,1)S(1)}) fusion(bf16[4,256,1024]{2,1,0:T(8,128)(2,1)} %bitcast.196), kind=kLoop, calls=%fused_computation.18 | loop fusion | bytes 4194304 | tf_op jit(solution)/shard_map/squeeze | solution.py:309
  81.5 4.3 %collective-permute-start.8 = (bf16[256,1024]{1,0:T(8,128)(2,1)S(1)}, bf16[256,1024]{1,0:T(8,128)(2,1)}, u32[]{:S(2)}, u32[]{:S(2)}) collective-permute-start(bf16[256,1024]{1,0:T(8,128)(2,1)S(1)} %get-tuple-element.59), channel_id=1, source_target_pairs={{0,8},{1,9},{2,10},{3,11},{4,12},{5,13},{6,14},{7,15},{8,16},{9,17... | collective-permute-start | bytes 1572872 | tf_op jit(solution)/shard_map/ppermute | solution.py:219
  85.8 6.0 %collective-permute-start.10 = (bf16[256,1024]{1,0:T(8,128)(2,1)S(1)}, bf16[256,1024]{1,0:T(8,128)(2,1)}, u32[]{:S(2)}, u32[]{:S(2)}) collective-permute-start(bf16[256,1024]{1,0:T(8,128)(2,1)S(1)} %get-tuple-element.58), channel_id=1, source_target_pairs={{0,16},{1,17},{2,18},{3,19},{4,20},{5,21},{6,22},{7,23},{8,24},{9,... | collective-permute-start | bytes 1572872 | tf_op jit(solution)/shard_map/ppermute | solution.py:219
  91.8 5.6 %collective-permute-start.11 = (bf16[256,1024]{1,0:T(8,128)(2,1)S(1)}, bf16[256,1024]{1,0:T(8,128)(2,1)}, u32[]{:S(2)}, u32[]{:S(2)}) collective-permute-start(bf16[256,1024]{1,0:T(8,128)(2,1)S(1)} %get-tuple-element.57), channel_id=1, source_target_pairs={{0,24},{1,25},{2,26},{3,27},{4,28},{5,29},{6,30},{7,31},{8,0},{9,1... | collective-permute-start | bytes 1572872 | tf_op jit(solution)/shard_map/ppermute | solution.py:219
  97.4 0.8 bitcast_dynamic-update-slice_fusion
  98.2 1.1 slice_bitcast_fusion.1
  99.3 3.4 %collective-permute-start.5 = (bf16[2,128,1024]{2,1,0:T(8,128)(2,1)S(1)}, bf16[2,128,1024]{2,1,0:T(8,128)(2,1)S(1)}, u32[]{:S(2)}, u32[]{:S(2)}) collective-permute-start(bf16[2,128,1024]{2,1,0:T(8,128)(2,1)S(1)} %slice_bitcast_fusion.1), channel_id=1, source_target_pairs={{0,64},{32,96},{64,128},{96,160},{128,192},{160,224},{192,0},{224,... | collective-permute-start | bytes 1572872 | tf_op jit(solution)/shard_map/ppermute | solution.py:219
  102.8 2.5 %collective-permute-start.7 = (bf16[2,128,1024]{2,1,0:T(8,128)(2,1)S(1)}, bf16[2,128,1024]{2,1,0:T(8,128)(2,1)S(1)}, u32[]{:S(2)}, u32[]{:S(2)}) collective-permute-start(bf16[2,128,1024]{2,1,0:T(8,128)(2,1)S(1)} %slice_bitcast_fusion), channel_id=1, source_target_pairs={{0,192},{32,224},{64,0},{96,32},{128,64},{160,96},{192,128},{224,1... | collective-permute-start | bytes 1572872 | tf_op jit(solution)/shard_map/ppermute | solution.py:219
  105.2 1.9 fusion.9
  107.1 1.9 fusion.8
  109.0 1.4 collective-permute-done.5
  110.4 0.9 fusion.7
  111.2 2.6 %collective-permute-done.7 = bf16[2,128,1024]{2,1,0:T(8,128)(2,1)S(1)} collective-permute-done((bf16[2,128,1024]{2,1,0:T(8,128)(2,1)S(1)}, bf16[2,128,1024]{2,1,0:T(8,128)(2,1)S(1)}, u32[]{:S(2)}, u32[]{:S(2)}) %collective-permute-start.7) | collective-permute-done | bytes 524320 | tf_op jit(solution)/shard_map/ppermute | solution.py:219
  113.8 0.8 fusion.6
  114.7 0.9 fusion.5
  115.5 0.9 fusion.4
  116.4 1.9 collective-permute-start.9
  118.3 13.6 %collective-permute-done.10.rest_2_ = bf16[256,1024]{1,0:T(8,128)(2,1)} collective-permute-done((bf16[256,1024]{1,0:T(8,128)(2,1)S(1)}, bf16[256,1024]{1,0:T(8,128)(2,1)}, u32[]{:S(2)}, u32[]{:S(2)}) %collective-permute-start.10) | collective-permute-done | bytes 524320 | tf_op jit(solution)/shard_map/ppermute | solution.py:219
  131.9 1.5 collective-permute-done.11.rest_3_
  133.4 1.9 collective-permute-start.12
  135.4 0.4 fusion
  135.7 0.9 convert_element_type.46.mask_ref
  136.6 0.3 select_reduce_fusion
  137.0 0.7 copy.13.mark_ref
  138.0 0.6 iota_add_fusion.mark_ref
  138.7 0.7 iota_add_fusion.1
  139.4 4.8 %exp_scores.2 = (f32[128,2048]{1,0:T(8,128)}, f32[128,1]{1,0:T(8,128)}) custom-call(bf16[128,1024]{1,0:T(8,128)(2,1)} %get-tuple-element.29.x_ref.q_ref, bf16[1024,1024]{1,0:T(8,128)(2,1)} %get-tuple-element.36.own_ref.own, bf16[1024,1024]{1,0:T(8,128)(2,1)} %collective-permute-done.9.other_ref.other), custom_call_target="tpu_custom_call" | custom-call | flops 536870912 | bytes 5505024 | tf_op jit(solution)/shard_map/exp_scores/pallas_call | solution.py:102
  144.3 1.3 copy-done
  145.6 3.5 %totals.1 = (f32[128,1]{1,0:T(8,128)}, bf16[128,1024]{1,0:T(8,128)(2,1)}, f32[1,1024]{1,0:T(1,128)}, f32[16,2,128]{2,1,0:T(2,128)}) custom-call(bf16[128,1024]{1,0:T(8,128)(2,1)} %get-tuple-element.29.x_ref.q_ref, bf16[1024,1024]{1,0:T(8,128)(2,1)} %bitcast.194, f32[128,1024]{1,0:T(8,128)} %convert_element_type.46.mask_ref, ...), custom_call_target="tpu_custom_call" | custom-call | flops 268435456 | bytes 2883584 | tf_op jit(solution)/shard_map/totals/pallas_call | solution.py:140
  149.1 5.1 %all-to-all-start.2 = ((f32[16,2,128]{2,1,0:T(2,128)}), f32[16,2,128]{2,1,0:T(2,128)S(1)}, u32[]{:S(2)}, u32[]{:S(2)}) async-start(f32[16,2,128]{2,1,0:T(2,128)} %get-tuple-element.40), calls=%async_computation.2 | async-start | bytes 32768 | tf_op jit(solution)/shard_map/all_to_all | solution.py:212
  154.2 0.5 broadcast.610
  154.7 1.3 reduce.3
  156.2 0.3 select_reduce_fusion.2
  156.4 4.8 %exp_scores.3 = (f32[128,2048]{1,0:T(8,128)}, f32[128,1]{1,0:T(8,128)}) custom-call(bf16[128,1024]{1,0:T(8,128)(2,1)} %get-tuple-element.30.x_ref, bf16[1024,1024]{1,0:T(8,128)(2,1)} %get-tuple-element.38.own_ref.own, bf16[1024,1024]{1,0:T(8,128)(2,1)} %collective-permute-done.12.other_ref.other), custom_call_target="tpu_custom_call" | custom-call | flops 536870912 | bytes 5505024 | tf_op jit(solution)/shard_map/exp_scores/pallas_call | solution.py:102
  161.2 0.6 gather_fusion
  161.8 0.6 fusion.26
  162.4 0.6 copy.14
  163.1 12.2 %all-to-all-start.3 = ((f32[32,2,32]{2,1,0:T(2,128)}), f32[32,2,32]{2,1,0:T(2,128)S(1)}, u32[]{:S(2)}, u32[]{:S(2)}) async-start(f32[32,2,32]{2,1,0:T(2,128)} %copy.14), calls=%async_computation.3 | async-start | bytes 65536 | tf_op jit(solution)/shard_map/all_to_all | solution.py:212
  175.3 5.6 %gradients.2 = bf16[128,1024]{1,0:T(8,128)(2,1)} custom-call(f32[128,2048]{1,0:T(8,128)} %get-tuple-element.44.exp_ref, f32[128,1]{1,0:T(8,128)} %get-tuple-element.45.total_ref, s32[128,1]{1,0:T(8,128)} %copy.13.mark_ref, s32[1,2048]{1,0:T(1,128)} %bitcast.208, bf16[1024,1024]{1,0:T(8,128)(2,1)} %get-tuple-element.36.own_ref.own, ...), custom_call_target="tpu_custom_call" | custom-call | flops 805306368 | bytes 8126464 | tf_op jit(solution)/shard_map/gradients/pallas_call | solution.py:192
  180.9 6.5 %all-to-all-done.3 = f32[32,2,32]{2,1,0:T(2,128)S(1)} async-done(((f32[32,2,32]{2,1,0:T(2,128)}), f32[32,2,32]{2,1,0:T(2,128)S(1)}, u32[]{:S(2)}, u32[]{:S(2)}) %all-to-all-start.3) | async-done | bytes 8224 | tf_op jit(solution)/shard_map/all_to_all | solution.py:212
  187.7 0.8 select_convert_fusion.w_ref
  188.4 5.5 %gradients.3 = bf16[128,1024]{1,0:T(8,128)(2,1)} custom-call(f32[128,2048]{1,0:T(8,128)} %get-tuple-element.49.exp_ref, f32[1,2048]{1,0:T(1,128)} %get-tuple-element.77.total_ref, s32[128,1]{1,0:T(8,128)} %iota_add_fusion.mark_ref, s32[1,2048]{1,0:T(1,128)} %get-tuple-element.76.marks_ref, bf16[1024,1024]{1,0:T(8,128)(2,1)} %get-tuple-element.38.own_ref.own, ...), custom_call_target="tpu_custom_call" | custom-call | flops 805306368 | bytes 8126464 | tf_op jit(solution)/shard_map/gradients/pallas_call | solution.py:192
  (56 shorter events, 1.4 us)
Async XLA Ops:
  7.2 51.6 %all-gather.2.cloned.1.call-start = ((), (), s32[]{:S(2)}) async-start(), calls=%async_computation.4 | async-start | bytes 2359296 | tf_op jit(solution)/shard_map/all_gather | solution.py:280
  9.4 36.8 %collective-permute-start.2 = (bf16[128,1024]{1,0:T(8,128)(2,1)}, bf16[128,1024]{1,0:T(8,128)(2,1)S(1)}, u32[]{:S(2)}, u32[]{:S(2)}) collective-permute-start(bf16[128,1024]{1,0:T(8,128)(2,1)} %get-tuple-element.30.x_ref), channel_id=1, source_target_pairs={{0,8},{1,9},{2,10},{3,11},{4,12},{5,13},{6,14},{7,15},{8,16},{9,17... | collective-permute-start | bytes 786440 | tf_op jit(solution)/shard_map/ppermute | solution.py:219
  15.5 30.7 %collective-permute-start.1 = (bf16[128,1024]{1,0:T(8,128)(2,1)}, bf16[128,1024]{1,0:T(8,128)(2,1)S(1)}, u32[]{:S(2)}, u32[]{:S(2)}) collective-permute-start(bf16[128,1024]{1,0:T(8,128)(2,1)} %get-tuple-element.30.x_ref), channel_id=1, source_target_pairs={{0,16},{1,17},{2,18},{3,19},{4,20},{5,21},{6,22},{7,23},{8,24},{9,... | collective-permute-start | bytes 786440 | tf_op jit(solution)/shard_map/ppermute | solution.py:219
  24.7 24.0 %collective-permute-start = (bf16[128,1024]{1,0:T(8,128)(2,1)}, bf16[128,1024]{1,0:T(8,128)(2,1)S(1)}, u32[]{:S(2)}, u32[]{:S(2)}) collective-permute-start(bf16[128,1024]{1,0:T(8,128)(2,1)} %get-tuple-element.30.x_ref), channel_id=1, source_target_pairs={{0,24},{1,25},{2,26},{3,27},{4,28},{5,29},{6,30},{7,31},{8,0},{9,1... | collective-permute-start | bytes 786440 | tf_op jit(solution)/shard_map/ppermute | solution.py:219
  29.6 15.0 %all-to-all-start = ((s32[8,1,512]{2,1,0:T(1,128)}), s32[8,1,512]{2,1,0:T(1,128)S(1)}, u32[]{:S(2)}, u32[]{:S(2)}) async-start(s32[8,1,512]{2,1,0:T(1,128)} %broadcast_in_dim.129), calls=%async_computation | async-start | bytes 32768 | tf_op jit(solution)/shard_map/all_to_all | solution.py:212
  36.7 28.7 %collective-permute-start.3 = (bf16[2,128,1024]{2,1,0:T(8,128)(2,1)}, bf16[2,128,1024]{2,1,0:T(8,128)(2,1)S(1)}, u32[]{:S(2)}, u32[]{:S(2)}) collective-permute-start(bf16[2,128,1024]{2,1,0:T(8,128)(2,1)} %get-tuple-element.32), channel_id=1, source_target_pairs={{0,256},{32,288},{64,320},{96,352},{128,384},{160,416},{192,448},{... | collective-permute-start | bytes 1572872 | tf_op jit(solution)/shard_map/ppermute | solution.py:219
  58.7 6.7 %copy-start.1 = (bf16[2,128,1024]{2,1,0:T(8,128)(2,1)S(1)}, bf16[2,128,1024]{2,1,0:T(8,128)(2,1)}, u32[]{:S(2)}) copy-start(bf16[2,128,1024]{2,1,0:T(8,128)(2,1)} %get-tuple-element.32) | copy-start | bytes 1572868
  65.4 4.6 %copy-start.4 = (s32[128,4]{0,1:T(4,128)S(1)}, s32[128,4]{0,1:T(4,128)}, u32[]{:S(2)}) copy-start(s32[128,4]{0,1:T(4,128)} %param.8) | copy-start | bytes 6148
  65.4 8.7 %copy-start.2 = (bf16[2,128,1024]{2,1,0:T(8,128)(2,1)}, bf16[2,128,1024]{2,1,0:T(8,128)(2,1)S(1)}, u32[]{:S(2)}) copy-start(bf16[2,128,1024]{2,1,0:T(8,128)(2,1)S(1)} %collective-permute-done.3) | copy-start | bytes 1572868
  66.6 31.7 %collective-permute-start.4 = (bf16[2,2,128,1024]{3,2,1,0:T(8,128)(2,1)}, bf16[2,2,128,1024]{3,2,1,0:T(8,128)(2,1)}, u32[]{:S(2)}, u32[]{:S(2)}) collective-permute-start(bf16[2,2,128,1024]{3,2,1,0:T(8,128)(2,1)} %pad_maximum_fusion.1), channel_id=1, source_target_pairs={{0,64},{32,96},{64,128},{96,160},{128,192},{160,224},{192,0},{224,... | collective-permute-start | bytes 3145736 | tf_op jit(solution)/shard_map/ppermute | solution.py:219
  70.2 32.5 %collective-permute-start.6 = (bf16[2,2,128,1024]{3,2,1,0:T(8,128)(2,1)}, bf16[2,2,128,1024]{3,2,1,0:T(8,128)(2,1)S(1)}, u32[]{:S(2)}, u32[]{:S(2)}) collective-permute-start(bf16[2,2,128,1024]{3,2,1,0:T(8,128)(2,1)} %pad_maximum_fusion.1), channel_id=1, source_target_pairs={{0,192},{32,224},{64,0},{96,32},{128,64},{160,96},{192,128},{224,1... | collective-permute-start | bytes 3145736 | tf_op jit(solution)/shard_map/ppermute | solution.py:219
  74.1 70.2 %all-to-all-start.1 = ((bf16[8,128,1024]{2,1,0:T(8,128)(2,1)}), bf16[8,128,1024]{2,1,0:T(8,128)(2,1)S(1)}, u32[]{:S(2)}, u32[]{:S(2)}) async-start(bf16[8,128,1024]{2,1,0:T(8,128)(2,1)} %bitcast.197), calls=%async_computation.1 | async-start | bytes 4194304 | tf_op jit(solution)/shard_map/all_to_all | solution.py:212
  78.9 18.5 %copy-start.3 = (bf16[2,128,1024]{2,1,0:T(8,128)(2,1)S(1)}, bf16[2,128,1024]{2,1,0:T(8,128)(2,1)}, u32[]{:S(2)}) copy-start(bf16[2,128,1024]{2,1,0:T(8,128)(2,1)} %copy-done.2) | copy-start | bytes 1572868
  81.5 34.8 %collective-permute-start.8 = (bf16[256,1024]{1,0:T(8,128)(2,1)S(1)}, bf16[256,1024]{1,0:T(8,128)(2,1)}, u32[]{:S(2)}, u32[]{:S(2)}) collective-permute-start(bf16[256,1024]{1,0:T(8,128)(2,1)S(1)} %get-tuple-element.59), channel_id=1, source_target_pairs={{0,8},{1,9},{2,10},{3,11},{4,12},{5,13},{6,14},{7,15},{8,16},{9,17... | collective-permute-start | bytes 1572872 | tf_op jit(solution)/shard_map/ppermute | solution.py:219
  85.8 46.1 %collective-permute-start.10 = (bf16[256,1024]{1,0:T(8,128)(2,1)S(1)}, bf16[256,1024]{1,0:T(8,128)(2,1)}, u32[]{:S(2)}, u32[]{:S(2)}) collective-permute-start(bf16[256,1024]{1,0:T(8,128)(2,1)S(1)} %get-tuple-element.58), channel_id=1, source_target_pairs={{0,16},{1,17},{2,18},{3,19},{4,20},{5,21},{6,22},{7,23},{8,24},{9,... | collective-permute-start | bytes 1572872 | tf_op jit(solution)/shard_map/ppermute | solution.py:219
  91.8 41.6 %collective-permute-start.11 = (bf16[256,1024]{1,0:T(8,128)(2,1)S(1)}, bf16[256,1024]{1,0:T(8,128)(2,1)}, u32[]{:S(2)}, u32[]{:S(2)}) collective-permute-start(bf16[256,1024]{1,0:T(8,128)(2,1)S(1)} %get-tuple-element.57), channel_id=1, source_target_pairs={{0,24},{1,25},{2,26},{3,27},{4,28},{5,29},{6,30},{7,31},{8,0},{9,1... | collective-permute-start | bytes 1572872 | tf_op jit(solution)/shard_map/ppermute | solution.py:219
  99.3 11.1 %collective-permute-start.5 = (bf16[2,128,1024]{2,1,0:T(8,128)(2,1)S(1)}, bf16[2,128,1024]{2,1,0:T(8,128)(2,1)S(1)}, u32[]{:S(2)}, u32[]{:S(2)}) collective-permute-start(bf16[2,128,1024]{2,1,0:T(8,128)(2,1)S(1)} %slice_bitcast_fusion.1), channel_id=1, source_target_pairs={{0,64},{32,96},{64,128},{96,160},{128,192},{160,224},{192,0},{224,... | collective-permute-start | bytes 1572872 | tf_op jit(solution)/shard_map/ppermute | solution.py:219
  102.8 11.1 %collective-permute-start.7 = (bf16[2,128,1024]{2,1,0:T(8,128)(2,1)S(1)}, bf16[2,128,1024]{2,1,0:T(8,128)(2,1)S(1)}, u32[]{:S(2)}, u32[]{:S(2)}) collective-permute-start(bf16[2,128,1024]{2,1,0:T(8,128)(2,1)S(1)} %slice_bitcast_fusion), channel_id=1, source_target_pairs={{0,192},{32,224},{64,0},{96,32},{128,64},{160,96},{192,128},{224,1... | collective-permute-start | bytes 1572872 | tf_op jit(solution)/shard_map/ppermute | solution.py:219
  110.4 24.9 %copy-start.6 = (s32[128]{0:T(128)S(1)}, s32[128]{0:T(128)}, u32[]{:S(2)}) copy-start(s32[128]{0:T(128)} %param.9) | copy-start | bytes 1540
  111.2 25.7 %copy-start.5 = (s32[128]{0:T(128)S(1)}, s32[128]{0:T(128)}, u32[]{:S(2)}) copy-start(s32[128]{0:T(128)} %param.7) | copy-start | bytes 1540
  116.4 23.0 %collective-permute-start.9 = (bf16[1024,1024]{1,0:T(8,128)(2,1)}, bf16[1024,1024]{1,0:T(8,128)(2,1)}, u32[]{:S(2)}, u32[]{:S(2)}) collective-permute-start(bf16[1024,1024]{1,0:T(8,128)(2,1)} %get-tuple-element.36.own_ref.own), channel_id=1, source_target_pairs={{0,32},{32,0},{64,96},{96,64},{128,160},{160,128},{192,224},{224,1... | collective-permute-start | bytes 6291464 | tf_op jit(solution)/shard_map/ppermute | solution.py:219
  133.4 10.9 %collective-permute-start.12 = (bf16[1024,1024]{1,0:T(8,128)(2,1)}, bf16[1024,1024]{1,0:T(8,128)(2,1)}, u32[]{:S(2)}, u32[]{:S(2)}) collective-permute-start(bf16[1024,1024]{1,0:T(8,128)(2,1)} %get-tuple-element.38.own_ref.own), channel_id=1, source_target_pairs={{0,32},{32,0},{64,96},{96,64},{128,160},{160,128},{192,224},{224,1... | collective-permute-start | bytes 6291464 | tf_op jit(solution)/shard_map/ppermute | solution.py:219
  144.2 1.3 copy-start
  149.1 12.1 %all-to-all-start.2 = ((f32[16,2,128]{2,1,0:T(2,128)}), f32[16,2,128]{2,1,0:T(2,128)S(1)}, u32[]{:S(2)}, u32[]{:S(2)}) async-start(f32[16,2,128]{2,1,0:T(2,128)} %get-tuple-element.40), calls=%async_computation.2 | async-start | bytes 32768 | tf_op jit(solution)/shard_map/all_to_all | solution.py:212
  163.1 24.3 %all-to-all-start.3 = ((f32[32,2,32]{2,1,0:T(2,128)}), f32[32,2,32]{2,1,0:T(2,128)S(1)}, u32[]{:S(2)}, u32[]{:S(2)}) async-start(f32[32,2,32]{2,1,0:T(2,128)} %copy.14), calls=%async_computation.3 | async-start | bytes 65536 | tf_op jit(solution)/shard_map/all_to_all | solution.py:212
Sparse Core Ops, SparseCore 0:
  10.7 48.0 all-gather.1

commit v2 on v1

--- a/solution.py
+++ b/solution.py
@@ -38,7 +38,7 @@
     )(queries, passages)
 
 
-def pick_kernel(index_ref, pool_ref, out_ref):
+def pick_kernel(index_ref, pool_ref, *out_refs):
     rows = pool_ref.shape[1]
     index = index_ref[0]
     pick = index == lax.broadcasted_iota(jnp.int32, (rows, index.shape[1]), 0)
@@ -48,12 +48,20 @@
         (((0,), (0,)), ((), ())),
         preferred_element_type=jnp.float32,
     )
-    out_ref[...] = found.astype(jnp.bfloat16).reshape(out_ref.shape)
-
-
-def pick_rows(index, pool):
+    found = found.astype(jnp.bfloat16)
+    at = 0
+    for out_ref in out_refs:
+        part = index.shape[1] // len(out_refs)
+        out_ref[...] = found[at : at + part].reshape(out_ref.shape)
+        at += part
+
+
+def pick_rows(index, pool, apart=False):
     groups, rows, width = pool.shape
     _, parts, ranks = index.shape
+    split = parts if apart else 1
+    block = (parts // split, 1, ranks, width)
+    whole = (parts // split, groups, ranks, width)
     found = pl.pallas_call(
         pick_kernel,
         grid=(groups,),
@@ -61,9 +69,9 @@
             pl.BlockSpec((1, 1, parts * ranks), lambda g: (g, 0, 0)),
             pl.BlockSpec((1, rows, width), lambda g: (g, 0, 0)),
         ],
-        out_specs=pl.BlockSpec((parts, 1, ranks, width), lambda g: (0, g, 0, 0)),
-        out_shape=jax.ShapeDtypeStruct((parts, groups, ranks, width), jnp.bfloat16),
-        compiler_params=ROOMY,
+        out_specs=[pl.BlockSpec(block, lambda g: (0, g, 0, 0))] * split,
+        out_shape=[jax.ShapeDtypeStruct(whole, jnp.bfloat16)] * split,
+        compiler_params=pltpu.CompilerParams(vmem_limit_bytes=4 * 1024 * 1024),
         cost_estimate=pl.CostEstimate(
             flops=2 * groups * rows * parts * ranks * width,
             bytes_accessed=2 * groups * (rows + parts * ranks) * width,
@@ -71,7 +79,9 @@
         ),
         name="pick_rows",
     )(index.reshape(groups, 1, parts * ranks), pool)
-    return found.reshape(parts, groups * ranks, width)
+    if apart:
+        return [part.reshape(groups * ranks, width) for part in found]
+    return found[0].reshape(parts, groups * ranks, width)
 
 
 TILE = 256
@@ -246,7 +256,7 @@
         return shifted(value, "blk", lambda i: beside(i, step, length))
 
     over = shifted(both, "blk", lambda i: (i + length // 2) % length)
-    over, after = lax.optimization_barrier((over, after))
+    over, *after = lax.optimization_barrier((over, *after))
     pair = jnp.stack([both, over])
     right = turned(pair, 1)
     left = turned(pair, -1)
@@ -303,17 +313,11 @@
 
     sent_p = pick_rows(asked_row, p_line)
     asked_by, sent_p = lax.optimization_barrier((asked_by, sent_p))
-    sent_q = pick_rows(jnp.swapaxes(asked_by, 0, 1), q_line.reshape(ny, rows, width))
+    sent_q = pick_rows(jnp.swapaxes(asked_by, 0, 1), q_line.reshape(ny, rows, width), True)
     got_p = exchange(sent_p, "dp", lines).reshape(slots, width)
     (p_own, q_own), sent_q = gather_chips(both, sent_q)
     got_q = [sent_q[0]]
     got_q += [shifted(sent_q[t], "dp", lambda i, t=t: along_z(i, t)) for t in range(1, nz)]
-
-    p_own, got_q[1] = lax.optimization_barrier((p_own, got_q[1]))
-    q_own, got_q[2], got_q[3] = lax.optimization_barrier((q_own, got_q[2], got_q[3]))
-    p_other = shifted(p_own, "blk", sibling)
-    q_other = shifted(q_own, "blk", sibling)
-    where = blk_order(me_blk)
 
     owner = own_ids // rows
     before = (owner[:, None] == owner[None, :]) & (number[None, :] < number[:, None])
@@ -328,12 +332,21 @@
     own_asked = jnp.sum(
         jnp.where(used_place[:, :, None] == slot[None, None, :], wanted, 0), axis=(0, 1)
     )
+    mask = weighs.astype(jnp.float32)
+
+    p_own, got_q[1], mask, own_asked = lax.optimization_barrier(
+        (p_own, got_q[1], mask, own_asked)
+    )
+    q_own, got_q[2], got_q[3] = lax.optimization_barrier((q_own, got_q[2], got_q[3]))
+    p_other = shifted(p_own, "blk", sibling)
+    q_other = shifted(q_own, "blk", sibling)
+    where = blk_order(me_blk)
 
     exp_scores, sums = exp_scores_of(q_half, p_own, p_other)
     sums, q_other = lax.optimization_barrier((sums, q_other))
     exp_back, _ = exp_scores_of(p_half, q_own, q_other)
     total, weights, slot_weights, facts = totals_of(
-        q_half, got_p, weighs.astype(jnp.float32), sums, positive, length
+        q_half, got_p, mask, sums, positive, length
     )
 
     peer = jnp.arange(peers, dtype=jnp.int32)

time: 202 us -> 198 us (0.980)
  Pallas kernels: 37.4 us -> 31.2 us
  waiting for transfers between devices: 35.4 us -> 38.7 us
    pallas_call x2, Pallas kernels: 10.9 us -> 4.68 us  [pick_rows(): pl.pallas_call(pick_kernel, grid=(groups,), in_specs=[pl.BlockSpec((1, 1,...]
    unnamed x21 -> x31, local copies, waits for them, and re-layouts: 9.34 us -> 12.6 us
    all_gather x1, waiting for transfers between devices: 3 us -> 6.23 us  [local(): lax.all_gather(q_half, 'dp', axis=0, tiled=True, axis_index_groups=lines)]
    squeeze x1 -> x0, local copies, waits for them, and re-layouts: 2.62 us -> none  [local(): got_q = [sent_q[0]]]
  transfers between devices with their start and end apart: 18 -> 18, of which waited for: 8 -> 8; matrix products, arithmetic and copies ran while one was open for 12% -> 11% of each run, Pallas kernels for 13% -> 10%
where the time goes in v2:
time: 198 us; the launch traced here: 197 us
  starting transfers between devices  82.9 us (42%)
  waiting for transfers between devices  38.7 us (20%)
  Pallas kernels  31.2 us (16%)
  local copies, waits for them, and re-layouts  19.2 us (10%)
  between operations  15 us (8%)
  other arithmetic  9.96 us (5%)
    ppermute x13, starting transfers between devices, shifted(): return lax.ppermute(value, axis, [(i, move(i)) for i in range(devices)])  53.7 us
    all_to_all x4, starting transfers between devices, exchange(): lax.all_to_all(value, axis, split_axis=0, concat_axis=0, tiled=True, axis...  29.1 us
    ppermute x13, waiting for transfers between devices, shifted(): return lax.ppermute(value, axis, [(i, move(i)) for i in range(devices)])  22.3 us
    unnamed x31, local copies, waits for them, and re-layouts  12.6 us
    pallas_call x2, Pallas kernels, grads_of(): pl.pallas_call(grad_kernel, in_specs=[whole] * len(operands) + [pl.BlockS...  11.1 us
    all_to_all x4, waiting for transfers between devices, exchange(): lax.all_to_all(value, axis, split_axis=0, concat_axis=0, tiled=True, axis...  10.2 us
    pallas_call x2, Pallas kernels, exp_scores_of(): pl.pallas_call(exp_kernel, out_shape=(jax.ShapeDtypeStruct((rows, 2 * own...  9.64 us
    all_gather x1, waiting for transfers between devices, local(): lax.all_gather(q_half, 'dp', axis=0, tiled=True, axis_index_groups=lines)  6.23 us
  transfers between devices with their start and end apart: 18, of which 8 were waited for; matrix products, arithmetic and copies ran while one was open for 11% of the time, Pallas kernels for 10%

profile of v2, /device:TPU:2, one launch (start us, length us, event | category | flops | bytes accessed | tf_op | source)
XLA Modules:
  0.0 197.1 jit_solution(7864266379695821509)
XLA Ops:
  7.2 2.2 %unit_halves.1 = (bf16[128,1024]{1,0:T(8,128)(2,1)}, bf16[128,1024]{1,0:T(8,128)(2,1)}, bf16[2,128,1024]{2,1,0:T(8,128)(2,1)}, f32[128,1]{1,0:T(8,128)}, f32[128,1]{1,0:T(8,128)}) custom-call(bf16[128,1024]{1,0:T(8,128)(2,1)} %x_ref.2, bf16[128,1024]{1,0:T(8,128)(2,1)} %x_ref.3), custom_call_target="tpu_custom_call" | custom-call | flops 1048576 | bytes 1572864 | tf_op jit(solution)/shard_map/unit_halves/pallas_call | solution.py:31
  9.4 6.1 %collective-permute-start.2 = (bf16[128,1024]{1,0:T(8,128)(2,1)}, bf16[128,1024]{1,0:T(8,128)(2,1)S(1)}, u32[]{:S(2)}, u32[]{:S(2)}) collective-permute-start(bf16[128,1024]{1,0:T(8,128)(2,1)} %get-tuple-element.39.x_ref), channel_id=1, source_target_pairs={{0,8},{1,9},{2,10},{3,11},{4,12},{5,13},{6,14},{7,15},{8,16},{9,17... | collective-permute-start | bytes 786440 | tf_op jit(solution)/shard_map/ppermute | solution.py:229
  15.5 9.1 %collective-permute-start.1 = (bf16[128,1024]{1,0:T(8,128)(2,1)}, bf16[128,1024]{1,0:T(8,128)(2,1)S(1)}, u32[]{:S(2)}, u32[]{:S(2)}) collective-permute-start(bf16[128,1024]{1,0:T(8,128)(2,1)} %get-tuple-element.39.x_ref), channel_id=1, source_target_pairs={{0,16},{1,17},{2,18},{3,19},{4,20},{5,21},{6,22},{7,23},{8,24},{9,... | collective-permute-start | bytes 786440 | tf_op jit(solution)/shard_map/ppermute | solution.py:229
  24.7 3.7 %collective-permute-start = (bf16[128,1024]{1,0:T(8,128)(2,1)}, bf16[128,1024]{1,0:T(8,128)(2,1)S(1)}, u32[]{:S(2)}, u32[]{:S(2)}) collective-permute-start(bf16[128,1024]{1,0:T(8,128)(2,1)} %get-tuple-element.39.x_ref), channel_id=1, source_target_pairs={{0,24},{1,25},{2,26},{3,27},{4,28},{5,29},{6,30},{7,31},{8,0},{9,1... | collective-permute-start | bytes 786440 | tf_op jit(solution)/shard_map/ppermute | solution.py:229
  28.3 1.3 broadcast_in_dim.129
  29.6 7.1 %all-to-all-start = ((s32[8,1,512]{2,1,0:T(1,128)}), s32[8,1,512]{2,1,0:T(1,128)S(1)}, u32[]{:S(2)}, u32[]{:S(2)}) async-start(s32[8,1,512]{2,1,0:T(1,128)} %broadcast_in_dim.129), calls=%async_computation | async-start | bytes 32768 | tf_op jit(solution)/shard_map/all_to_all | solution.py:222
  36.7 3.4 %collective-permute-start.3 = (bf16[2,128,1024]{2,1,0:T(8,128)(2,1)}, bf16[2,128,1024]{2,1,0:T(8,128)(2,1)S(1)}, u32[]{:S(2)}, u32[]{:S(2)}) collective-permute-start(bf16[2,128,1024]{2,1,0:T(8,128)(2,1)} %get-tuple-element.41), channel_id=1, source_target_pairs={{0,256},{32,288},{64,320},{96,352},{128,384},{160,416},{192,448},{... | collective-permute-start | bytes 1572872 | tf_op jit(solution)/shard_map/ppermute | solution.py:229
  40.1 0.7 add_select_fusion.4
  41.0 3.6 %all-to-all-done = s32[8,1,512]{2,1,0:T(1,128)S(1)} async-done(((s32[8,1,512]{2,1,0:T(1,128)}), s32[8,1,512]{2,1,0:T(1,128)S(1)}, u32[]{:S(2)}, u32[]{:S(2)}) %all-to-all-start) | async-done | bytes 16416 | tf_op jit(solution)/shard_map/all_to_all | solution.py:222
  44.9 0.6 select_reduce_fusion.1
  45.7 3.0 %collective-permute-done = bf16[128,1024]{1,0:T(8,128)(2,1)S(1)} collective-permute-done((bf16[128,1024]{1,0:T(8,128)(2,1)}, bf16[128,1024]{1,0:T(8,128)(2,1)S(1)}, u32[]{:S(2)}, u32[]{:S(2)}) %collective-permute-start) | collective-permute-done | bytes 262176 | tf_op jit(solution)/shard_map/ppermute | solution.py:229
  48.7 1.1 pad_maximum_fusion.pool_ref
  49.8 2.6 %pick_rows.2 = bf16[8,4,32,1024]{3,2,1,0:T(8,128)(2,1)} custom-call(s32[4,1,256]{2,1,0:T(1,128)S(1)} %fusion.27.index_ref, bf16[4,128,1024]{2,1,0:T(8,128)(2,1)S(1)} %pad_maximum_fusion.pool_ref), custom_call_target="tpu_custom_call" | custom-call | flops 268435456 | bytes 3145728 | tf_op jit(solution)/shard_map/pick_rows/pallas_call | solution.py:65
  52.5 6.2 %all-gather.2.cloned.1.call-done = bf16[1024,1024]{1,0:T(8,128)(2,1)} async-done(((bf16[128,1024]{1,0:T(8,128)(2,1)}), bf16[1024,1024]{1,0:T(8,128)(2,1)}) %all-gather.2.cloned.1.call-update) | async-done | bytes 2097168 | tf_op jit(solution)/shard_map/all_gather | solution.py:290
  58.7 1.6 copy-done
  60.3 2.1 %pick_rows.3 = (bf16[1,8,32,1024]{3,2,1,0:T(8,128)(2,1)S(1)}, bf16[1,8,32,1024]{3,2,1,0:T(8,128)(2,1)S(1)}, bf16[1,8,32,1024]{3,2,1,0:T(8,128)(2,1)S(1)}, bf16[1,8,32,1024]{3,2,1,0:T(8,128)(2,1)S(1)}) custom-call(s32[8,1,128]{2,1,0:T(1,128)S(1)} %reshape.1214.index_ref, bf16[8,128,1024]{2,1,0:T(8,128)(2,1)S(1)} %bitcast.189), custom_call_target="tpu_custom_call" | custom-call | flops 268435456 | bytes 4194304 | tf_op jit(solution)/shard_map/pick_rows/pallas_call | solution.py:65
  62.4 0.8 copy-done.1
  63.2 1.2 pad_maximum_fusion.1
  64.4 3.4 %collective-permute-start.4 = (bf16[2,2,128,1024]{3,2,1,0:T(8,128)(2,1)}, bf16[2,2,128,1024]{3,2,1,0:T(8,128)(2,1)}, u32[]{:S(2)}, u32[]{:S(2)}) collective-permute-start(bf16[2,2,128,1024]{3,2,1,0:T(8,128)(2,1)} %pad_maximum_fusion.1), channel_id=1, source_target_pairs={{0,64},{32,96},{64,128},{96,160},{128,192},{160,224},{192,0},{224,... | collective-permute-start | bytes 3145736 | tf_op jit(solution)/shard_map/ppermute | solution.py:229
  68.0 2.5 %collective-permute-start.6 = (bf16[2,2,128,1024]{3,2,1,0:T(8,128)(2,1)}, bf16[2,2,128,1024]{3,2,1,0:T(8,128)(2,1)S(1)}, u32[]{:S(2)}, u32[]{:S(2)}) collective-permute-start(bf16[2,2,128,1024]{3,2,1,0:T(8,128)(2,1)} %pad_maximum_fusion.1), channel_id=1, source_target_pairs={{0,192},{32,224},{64,0},{96,32},{128,64},{160,96},{192,128},{224,1... | collective-permute-start | bytes 3145736 | tf_op jit(solution)/shard_map/ppermute | solution.py:229
  70.5 0.4 fusion
  70.9 0.9 convert_element_type.35.mask_ref
  71.8 0.3 select_reduce_fusion
  72.1 0.9 bitcast_dynamic-update-slice_fusion.1
  73.0 5.0 %all-to-all-start.1 = ((bf16[8,128,1024]{2,1,0:T(8,128)(2,1)}), bf16[8,128,1024]{2,1,0:T(8,128)(2,1)}, u32[]{:S(2)}, u32[]{:S(2)}) async-start(bf16[8,128,1024]{2,1,0:T(8,128)(2,1)} %bitcast.8), calls=%async_computation.1 | async-start | bytes 4194304 | tf_op jit(solution)/shard_map/all_to_all | solution.py:222
  78.0 4.3 %collective-permute-start.8 = (bf16[256,1024]{1,0:T(8,128)(2,1)S(1)}, bf16[256,1024]{1,0:T(8,128)(2,1)S(1)}, u32[]{:S(2)}, u32[]{:S(2)}) collective-permute-start(bf16[256,1024]{1,0:T(8,128)(2,1)S(1)} %bitcast.193), channel_id=1, source_target_pairs={{0,8},{1,9},{2,10},{3,11},{4,12},{5,13},{6,14},{7,15},{8,16},{9,17... | collective-permute-start | bytes 1572872 | tf_op jit(solution)/shard_map/ppermute | solution.py:229
  82.3 6.1 %collective-permute-start.10 = (bf16[256,1024]{1,0:T(8,128)(2,1)S(1)}, bf16[256,1024]{1,0:T(8,128)(2,1)S(1)}, u32[]{:S(2)}, u32[]{:S(2)}) collective-permute-start(bf16[256,1024]{1,0:T(8,128)(2,1)S(1)} %bitcast.192), channel_id=1, source_target_pairs={{0,16},{1,17},{2,18},{3,19},{4,20},{5,21},{6,22},{7,23},{8,24},{9,... | collective-permute-start | bytes 1572872 | tf_op jit(solution)/shard_map/ppermute | solution.py:229
  88.4 5.6 %collective-permute-start.11 = (bf16[256,1024]{1,0:T(8,128)(2,1)S(1)}, bf16[256,1024]{1,0:T(8,128)(2,1)S(1)}, u32[]{:S(2)}, u32[]{:S(2)}) collective-permute-start(bf16[256,1024]{1,0:T(8,128)(2,1)S(1)} %bitcast.191), channel_id=1, source_target_pairs={{0,24},{1,25},{2,26},{3,27},{4,28},{5,29},{6,30},{7,31},{8,0},{9,1... | collective-permute-start | bytes 1572872 | tf_op jit(solution)/shard_map/ppermute | solution.py:229
  94.0 0.9 bitcast_dynamic-update-slice_fusion
  94.9 1.1 slice_bitcast_fusion.1
  96.0 3.4 %collective-permute-start.5 = (bf16[2,128,1024]{2,1,0:T(8,128)(2,1)S(1)}, bf16[2,128,1024]{2,1,0:T(8,128)(2,1)S(1)}, u32[]{:S(2)}, u32[]{:S(2)}) collective-permute-start(bf16[2,128,1024]{2,1,0:T(8,128)(2,1)S(1)} %slice_bitcast_fusion.1), channel_id=1, source_target_pairs={{0,64},{32,96},{64,128},{96,160},{128,192},{160,224},{192,0},{224,... | collective-permute-start | bytes 1572872 | tf_op jit(solution)/shard_map/ppermute | solution.py:229
  99.4 2.4 %collective-permute-start.7 = (bf16[2,128,1024]{2,1,0:T(8,128)(2,1)S(1)}, bf16[2,128,1024]{2,1,0:T(8,128)(2,1)S(1)}, u32[]{:S(2)}, u32[]{:S(2)}) collective-permute-start(bf16[2,128,1024]{2,1,0:T(8,128)(2,1)S(1)} %slice_bitcast_fusion), channel_id=1, source_target_pairs={{0,192},{32,224},{64,0},{96,32},{128,64},{160,96},{192,128},{224,1... | collective-permute-start | bytes 1572872 | tf_op jit(solution)/shard_map/ppermute | solution.py:229
  101.9 1.9 fusion.9
  103.8 1.9 fusion.8
  105.6 1.4 collective-permute-done.5
  107.0 0.9 fusion.7
  107.9 2.6 %collective-permute-done.7 = bf16[2,128,1024]{2,1,0:T(8,128)(2,1)S(1)} collective-permute-done((bf16[2,128,1024]{2,1,0:T(8,128)(2,1)S(1)}, bf16[2,128,1024]{2,1,0:T(8,128)(2,1)S(1)}, u32[]{:S(2)}, u32[]{:S(2)}) %collective-permute-start.7) | collective-permute-done | bytes 524320 | tf_op jit(solution)/shard_map/ppermute | solution.py:229
  110.5 0.9 fusion.6
  111.4 0.9 fusion.5
  112.2 0.8 fusion.4
  113.1 1.9 collective-permute-start.9
  115.0 5.0 %collective-permute-done.10.rest_2_ = bf16[256,1024]{1,0:T(8,128)(2,1)S(1)} collective-permute-done((bf16[256,1024]{1,0:T(8,128)(2,1)S(1)}, bf16[256,1024]{1,0:T(8,128)(2,1)S(1)}, u32[]{:S(2)}, u32[]{:S(2)}) %collective-permute-start.10) | collective-permute-done | bytes 524320 | tf_op jit(solution)/shard_map/ppermute | solution.py:229
  120.0 10.3 %collective-permute-done.11.rest_3_ = bf16[256,1024]{1,0:T(8,128)(2,1)S(1)} collective-permute-done((bf16[256,1024]{1,0:T(8,128)(2,1)S(1)}, bf16[256,1024]{1,0:T(8,128)(2,1)S(1)}, u32[]{:S(2)}, u32[]{:S(2)}) %collective-permute-start.11) | collective-permute-done | bytes 524320 | tf_op jit(solution)/shard_map/ppermute | solution.py:229
  130.3 0.8 copy-done.8
  131.1 1.9 collective-permute-start.12
  133.5 0.7 copy.13.mark_ref
  134.5 0.6 iota_add_fusion.mark_ref
  135.2 0.7 iota_add_fusion.1
  136.0 1.4 copy-done.2
  137.4 4.8 %exp_scores.2 = (f32[128,2048]{1,0:T(8,128)}, f32[128,1]{1,0:T(8,128)}) custom-call(bf16[128,1024]{1,0:T(8,128)(2,1)} %get-tuple-element.38.x_ref.q_ref, bf16[1024,1024]{1,0:T(8,128)(2,1)} %get-tuple-element.50.own_ref.own, bf16[1024,1024]{1,0:T(8,128)(2,1)} %copy-done.2), custom_call_target="tpu_custom_call" | custom-call | flops 536870912 | bytes 5505024 | tf_op jit(solution)/shard_map/exp_scores/pallas_call | solution.py:112
  142.2 3.5 %totals.1 = (f32[128,1]{1,0:T(8,128)}, bf16[128,1024]{1,0:T(8,128)(2,1)}, f32[1,1024]{1,0:T(1,128)}, f32[16,2,128]{2,1,0:T(2,128)}) custom-call(bf16[128,1024]{1,0:T(8,128)(2,1)} %get-tuple-element.38.x_ref.q_ref, bf16[1024,1024]{1,0:T(8,128)(2,1)} %bitcast.9.hard_ref.rest_0_, f32[128,1024]{1,0:T(8,128)} %convert_element_type.35.mask_ref, ...), custom_call_target="tpu_custom_call" | custom-call | flops 268435456 | bytes 2883584 | tf_op jit(solution)/shard_map/totals/pallas_call | solution.py:150
  145.7 5.1 %all-to-all-start.2 = ((f32[16,2,128]{2,1,0:T(2,128)}), f32[16,2,128]{2,1,0:T(2,128)S(1)}, u32[]{:S(2)}, u32[]{:S(2)}) async-start(f32[16,2,128]{2,1,0:T(2,128)} %get-tuple-element.56), calls=%async_computation.2 | async-start | bytes 32768 | tf_op jit(solution)/shard_map/all_to_all | solution.py:222
  150.8 0.5 broadcast.610
  151.3 1.3 reduce.3
  152.8 0.3 select_reduce_fusion.2
  153.0 4.8 %exp_scores.3 = (f32[128,2048]{1,0:T(8,128)}, f32[128,1]{1,0:T(8,128)}) custom-call(bf16[128,1024]{1,0:T(8,128)(2,1)} %get-tuple-element.39.x_ref, bf16[1024,1024]{1,0:T(8,128)(2,1)} %get-tuple-element.54.own_ref.own, bf16[1024,1024]{1,0:T(8,128)(2,1)} %collective-permute-done.12.other_ref.other), custom_call_target="tpu_custom_call" | custom-call | flops 536870912 | bytes 5505024 | tf_op jit(solution)/shard_map/exp_scores/pallas_call | solution.py:112
  157.9 0.6 gather_fusion
  158.4 0.6 fusion.26
  159.1 0.6 copy.14
  159.7 11.9 %all-to-all-start.3 = ((f32[32,2,32]{2,1,0:T(2,128)}), f32[32,2,32]{2,1,0:T(2,128)S(1)}, u32[]{:S(2)}, u32[]{:S(2)}) async-start(f32[32,2,32]{2,1,0:T(2,128)} %copy.14), calls=%async_computation.3 | async-start | bytes 65536 | tf_op jit(solution)/shard_map/all_to_all | solution.py:222
  171.6 5.6 %gradients.2 = bf16[128,1024]{1,0:T(8,128)(2,1)} custom-call(f32[128,2048]{1,0:T(8,128)} %get-tuple-element.61.exp_ref, f32[128,1]{1,0:T(8,128)} %get-tuple-element.62.total_ref, s32[128,1]{1,0:T(8,128)} %copy.13.mark_ref, s32[1,2048]{1,0:T(1,128)} %bitcast.203, bf16[1024,1024]{1,0:T(8,128)(2,1)} %get-tuple-element.50.own_ref.own, ...), custom_call_target="tpu_custom_call" | custom-call | flops 805306368 | bytes 8126464 | tf_op jit(solution)/shard_map/gradients/pallas_call | solution.py:202
  177.2 6.5 %all-to-all-done.3 = f32[32,2,32]{2,1,0:T(2,128)S(1)} async-done(((f32[32,2,32]{2,1,0:T(2,128)}), f32[32,2,32]{2,1,0:T(2,128)S(1)}, u32[]{:S(2)}, u32[]{:S(2)}) %all-to-all-start.3) | async-done | bytes 8224 | tf_op jit(solution)/shard_map/all_to_all | solution.py:222
  184.0 0.8 select_convert_fusion.w_ref
  184.7 5.5 %gradients.3 = bf16[128,1024]{1,0:T(8,128)(2,1)} custom-call(f32[128,2048]{1,0:T(8,128)} %get-tuple-element.66.exp_ref, f32[1,2048]{1,0:T(1,128)} %get-tuple-element.91.total_ref, s32[128,1]{1,0:T(8,128)} %iota_add_fusion.mark_ref, s32[1,2048]{1,0:T(1,128)} %get-tuple-element.90.marks_ref, bf16[1024,1024]{1,0:T(8,128)(2,1)} %get-tuple-element.54.own_ref.own, ...), custom_call_target="tpu_custom_call" | custom-call | flops 805306368 | bytes 8126464 | tf_op jit(solution)/shard_map/gradients/pallas_call | solution.py:202
  (65 shorter events, 1.8 us)
Async XLA Ops:
  7.2 51.6 %all-gather.2.cloned.1.call-start = ((), (), s32[]{:S(2)}) async-start(), calls=%async_computation.4 | async-start | bytes 2359296 | tf_op jit(solution)/shard_map/all_gather | solution.py:290
  9.4 36.2 %collective-permute-start.2 = (bf16[128,1024]{1,0:T(8,128)(2,1)}, bf16[128,1024]{1,0:T(8,128)(2,1)S(1)}, u32[]{:S(2)}, u32[]{:S(2)}) collective-permute-start(bf16[128,1024]{1,0:T(8,128)(2,1)} %get-tuple-element.39.x_ref), channel_id=1, source_target_pairs={{0,8},{1,9},{2,10},{3,11},{4,12},{5,13},{6,14},{7,15},{8,16},{9,17... | collective-permute-start | bytes 786440 | tf_op jit(solution)/shard_map/ppermute | solution.py:229
  15.5 30.1 %collective-permute-start.1 = (bf16[128,1024]{1,0:T(8,128)(2,1)}, bf16[128,1024]{1,0:T(8,128)(2,1)S(1)}, u32[]{:S(2)}, u32[]{:S(2)}) collective-permute-start(bf16[128,1024]{1,0:T(8,128)(2,1)} %get-tuple-element.39.x_ref), channel_id=1, source_target_pairs={{0,16},{1,17},{2,18},{3,19},{4,20},{5,21},{6,22},{7,23},{8,24},{9,... | collective-permute-start | bytes 786440 | tf_op jit(solution)/shard_map/ppermute | solution.py:229
  24.7 24.0 %collective-permute-start = (bf16[128,1024]{1,0:T(8,128)(2,1)}, bf16[128,1024]{1,0:T(8,128)(2,1)S(1)}, u32[]{:S(2)}, u32[]{:S(2)}) collective-permute-start(bf16[128,1024]{1,0:T(8,128)(2,1)} %get-tuple-element.39.x_ref), channel_id=1, source_target_pairs={{0,24},{1,25},{2,26},{3,27},{4,28},{5,29},{6,30},{7,31},{8,0},{9,1... | collective-permute-start | bytes 786440 | tf_op jit(solution)/shard_map/ppermute | solution.py:229
  29.6 15.0 %all-to-all-start = ((s32[8,1,512]{2,1,0:T(1,128)}), s32[8,1,512]{2,1,0:T(1,128)S(1)}, u32[]{:S(2)}, u32[]{:S(2)}) async-start(s32[8,1,512]{2,1,0:T(1,128)} %broadcast_in_dim.129), calls=%async_computation | async-start | bytes 32768 | tf_op jit(solution)/shard_map/all_to_all | solution.py:222
  36.7 26.5 %collective-permute-start.3 = (bf16[2,128,1024]{2,1,0:T(8,128)(2,1)}, bf16[2,128,1024]{2,1,0:T(8,128)(2,1)S(1)}, u32[]{:S(2)}, u32[]{:S(2)}) collective-permute-start(bf16[2,128,1024]{2,1,0:T(8,128)(2,1)} %get-tuple-element.41), channel_id=1, source_target_pairs={{0,256},{32,288},{64,320},{96,352},{128,384},{160,416},{192,448},{... | collective-permute-start | bytes 1572872 | tf_op jit(solution)/shard_map/ppermute | solution.py:229
  49.8 13.4 %copy-start.3 = (bf16[2,128,1024]{2,1,0:T(8,128)(2,1)S(1)}, bf16[2,128,1024]{2,1,0:T(8,128)(2,1)}, u32[]{:S(2)}) copy-start(bf16[2,128,1024]{2,1,0:T(8,128)(2,1)} %get-tuple-element.41) | copy-start | bytes 1572868
  58.7 1.6 copy-start
  60.3 10.2 %copy-start.9 = (s32[128,4]{0,1:T(4,128)S(1)}, s32[128,4]{0,1:T(4,128)}, u32[]{:S(2)}) copy-start(s32[128,4]{0,1:T(4,128)} %param.8) | copy-start | bytes 6148
  60.3 10.2 %copy-start.11 = (s32[128]{0:T(128)S(1)}, s32[128]{0:T(128)}, u32[]{:S(2)}) copy-start(s32[128]{0:T(128)} %param.9) | copy-start | bytes 1540
  62.4 0.8 copy-start.1
  63.2 4.6 %copy-start.4 = (bf16[2,128,1024]{2,1,0:T(8,128)(2,1)}, bf16[2,128,1024]{2,1,0:T(8,128)(2,1)S(1)}, u32[]{:S(2)}) copy-start(bf16[2,128,1024]{2,1,0:T(8,128)(2,1)S(1)} %collective-permute-done.3) | copy-start | bytes 1572868
  64.4 30.5 %collective-permute-start.4 = (bf16[2,2,128,1024]{3,2,1,0:T(8,128)(2,1)}, bf16[2,2,128,1024]{3,2,1,0:T(8,128)(2,1)}, u32[]{:S(2)}, u32[]{:S(2)}) collective-permute-start(bf16[2,2,128,1024]{3,2,1,0:T(8,128)(2,1)} %pad_maximum_fusion.1), channel_id=1, source_target_pairs={{0,64},{32,96},{64,128},{96,160},{128,192},{160,224},{192,0},{224,... | collective-permute-start | bytes 3145736 | tf_op jit(solution)/shard_map/ppermute | solution.py:229
  68.0 31.4 %collective-permute-start.6 = (bf16[2,2,128,1024]{3,2,1,0:T(8,128)(2,1)}, bf16[2,2,128,1024]{3,2,1,0:T(8,128)(2,1)S(1)}, u32[]{:S(2)}, u32[]{:S(2)}) collective-permute-start(bf16[2,2,128,1024]{3,2,1,0:T(8,128)(2,1)} %pad_maximum_fusion.1), channel_id=1, source_target_pairs={{0,192},{32,224},{64,0},{96,32},{128,64},{160,96},{192,128},{224,1... | collective-permute-start | bytes 3145736 | tf_op jit(solution)/shard_map/ppermute | solution.py:229
  73.0 21.1 %copy-start.5 = (bf16[2,128,1024]{2,1,0:T(8,128)(2,1)S(1)}, bf16[2,128,1024]{2,1,0:T(8,128)(2,1)}, u32[]{:S(2)}) copy-start(bf16[2,128,1024]{2,1,0:T(8,128)(2,1)} %copy-done.4) | copy-start | bytes 1572868
  73.0 69.2 %all-to-all-start.1 = ((bf16[8,128,1024]{2,1,0:T(8,128)(2,1)}), bf16[8,128,1024]{2,1,0:T(8,128)(2,1)}, u32[]{:S(2)}, u32[]{:S(2)}) async-start(bf16[8,128,1024]{2,1,0:T(8,128)(2,1)} %bitcast.8), calls=%async_computation.1 | async-start | bytes 4194304 | tf_op jit(solution)/shard_map/all_to_all | solution.py:222
  78.0 35.1 %collective-permute-start.8 = (bf16[256,1024]{1,0:T(8,128)(2,1)S(1)}, bf16[256,1024]{1,0:T(8,128)(2,1)S(1)}, u32[]{:S(2)}, u32[]{:S(2)}) collective-permute-start(bf16[256,1024]{1,0:T(8,128)(2,1)S(1)} %bitcast.193), channel_id=1, source_target_pairs={{0,8},{1,9},{2,10},{3,11},{4,12},{5,13},{6,14},{7,15},{8,16},{9,17... | collective-permute-start | bytes 1572872 | tf_op jit(solution)/shard_map/ppermute | solution.py:229
  82.3 37.7 %collective-permute-start.10 = (bf16[256,1024]{1,0:T(8,128)(2,1)S(1)}, bf16[256,1024]{1,0:T(8,128)(2,1)S(1)}, u32[]{:S(2)}, u32[]{:S(2)}) collective-permute-start(bf16[256,1024]{1,0:T(8,128)(2,1)S(1)} %bitcast.192), channel_id=1, source_target_pairs={{0,16},{1,17},{2,18},{3,19},{4,20},{5,21},{6,22},{7,23},{8,24},{9,... | collective-permute-start | bytes 1572872 | tf_op jit(solution)/shard_map/ppermute | solution.py:229
  88.4 41.8 %collective-permute-start.11 = (bf16[256,1024]{1,0:T(8,128)(2,1)S(1)}, bf16[256,1024]{1,0:T(8,128)(2,1)S(1)}, u32[]{:S(2)}, u32[]{:S(2)}) collective-permute-start(bf16[256,1024]{1,0:T(8,128)(2,1)S(1)} %bitcast.191), channel_id=1, source_target_pairs={{0,24},{1,25},{2,26},{3,27},{4,28},{5,29},{6,30},{7,31},{8,0},{9,1... | collective-permute-start | bytes 1572872 | tf_op jit(solution)/shard_map/ppermute | solution.py:229
  96.0 11.1 %collective-permute-start.5 = (bf16[2,128,1024]{2,1,0:T(8,128)(2,1)S(1)}, bf16[2,128,1024]{2,1,0:T(8,128)(2,1)S(1)}, u32[]{:S(2)}, u32[]{:S(2)}) collective-permute-start(bf16[2,128,1024]{2,1,0:T(8,128)(2,1)S(1)} %slice_bitcast_fusion.1), channel_id=1, source_target_pairs={{0,64},{32,96},{64,128},{96,160},{128,192},{160,224},{192,0},{224,... | collective-permute-start | bytes 1572872 | tf_op jit(solution)/shard_map/ppermute | solution.py:229
  99.4 11.1 %collective-permute-start.7 = (bf16[2,128,1024]{2,1,0:T(8,128)(2,1)S(1)}, bf16[2,128,1024]{2,1,0:T(8,128)(2,1)S(1)}, u32[]{:S(2)}, u32[]{:S(2)}) collective-permute-start(bf16[2,128,1024]{2,1,0:T(8,128)(2,1)S(1)} %slice_bitcast_fusion), channel_id=1, source_target_pairs={{0,192},{32,224},{64,0},{96,32},{128,64},{160,96},{192,128},{224,1... | collective-permute-start | bytes 1572872 | tf_op jit(solution)/shard_map/ppermute | solution.py:229
  107.9 25.6 %copy-start.10 = (s32[128]{0:T(128)S(1)}, s32[128]{0:T(128)}, u32[]{:S(2)}) copy-start(s32[128]{0:T(128)} %param.7) | copy-start | bytes 1540
  113.1 17.2 %copy-start.6 = (bf16[256,1024]{1,0:T(8,128)(2,1)}, bf16[256,1024]{1,0:T(8,128)(2,1)S(1)}, u32[]{:S(2)}) copy-start(bf16[256,1024]{1,0:T(8,128)(2,1)S(1)} %collective-permute-done.8.rest_1_) | copy-start | bytes 1572868
  113.1 22.9 %collective-permute-start.9 = (bf16[1024,1024]{1,0:T(8,128)(2,1)}, bf16[1024,1024]{1,0:T(8,128)(2,1)S(1)}, u32[]{:S(2)}, u32[]{:S(2)}) collective-permute-start(bf16[1024,1024]{1,0:T(8,128)(2,1)} %get-tuple-element.50.own_ref.own), channel_id=1, source_target_pairs={{0,32},{32,0},{64,96},{96,64},{128,160},{160,128},{192,224},{224,1... | collective-permute-start | bytes 6291464 | tf_op jit(solution)/shard_map/ppermute | solution.py:229
  120.0 10.3 %copy-start.7 = (bf16[256,1024]{1,0:T(8,128)(2,1)}, bf16[256,1024]{1,0:T(8,128)(2,1)S(1)}, u32[]{:S(2)}) copy-start(bf16[256,1024]{1,0:T(8,128)(2,1)S(1)} %collective-permute-done.10.rest_2_) | copy-start | bytes 1572868
  130.3 0.8 copy-start.8
  131.1 11.1 %collective-permute-start.12 = (bf16[1024,1024]{1,0:T(8,128)(2,1)}, bf16[1024,1024]{1,0:T(8,128)(2,1)}, u32[]{:S(2)}, u32[]{:S(2)}) collective-permute-start(bf16[1024,1024]{1,0:T(8,128)(2,1)} %get-tuple-element.54.own_ref.own), channel_id=1, source_target_pairs={{0,32},{32,0},{64,96},{96,64},{128,160},{160,128},{192,224},{224,1... | collective-permute-start | bytes 6291464 | tf_op jit(solution)/shard_map/ppermute | solution.py:229
  136.0 1.4 copy-start.2
  145.7 12.1 %all-to-all-start.2 = ((f32[16,2,128]{2,1,0:T(2,128)}), f32[16,2,128]{2,1,0:T(2,128)S(1)}, u32[]{:S(2)}, u32[]{:S(2)}) async-start(f32[16,2,128]{2,1,0:T(2,128)} %get-tuple-element.56), calls=%async_computation.2 | async-start | bytes 32768 | tf_op jit(solution)/shard_map/all_to_all | solution.py:222
  159.7 24.0 %all-to-all-start.3 = ((f32[32,2,32]{2,1,0:T(2,128)}), f32[32,2,32]{2,1,0:T(2,128)S(1)}, u32[]{:S(2)}, u32[]{:S(2)}) async-start(f32[32,2,32]{2,1,0:T(2,128)} %copy.14), calls=%async_computation.3 | async-start | bytes 65536 | tf_op jit(solution)/shard_map/all_to_all | solution.py:222
Sparse Core Ops, SparseCore 0:
  10.7 48.0 all-gather.1

commit v3 on v2

--- a/solution.py
+++ b/solution.py
@@ -249,7 +249,7 @@
     return jnp.stack(where)
 
 
-def gather_chips(both, after):
+def gather_chips(both, after, send):
     length = lax.axis_size("blk")
 
     def turned(value, step):
@@ -260,6 +260,8 @@
     pair = jnp.stack([both, over])
     right = turned(pair, 1)
     left = turned(pair, -1)
+    after = send(after)
+    right, left, after[1] = lax.optimization_barrier((right, left, after[1]))
     far = (turned(right[0], 1), turned(left[1], -1))
     blocks = (both, over, right[0], right[1], far[0], far[1], left[0], left[1])
     return [jnp.concatenate([block[k] for block in blocks]) for k in range(2)], after
@@ -315,9 +317,12 @@
     asked_by, sent_p = lax.optimization_barrier((asked_by, sent_p))
     sent_q = pick_rows(jnp.swapaxes(asked_by, 0, 1), q_line.reshape(ny, rows, width), True)
     got_p = exchange(sent_p, "dp", lines).reshape(slots, width)
-    (p_own, q_own), sent_q = gather_chips(both, sent_q)
-    got_q = [sent_q[0]]
-    got_q += [shifted(sent_q[t], "dp", lambda i, t=t: along_z(i, t)) for t in range(1, nz)]
+
+    def send(chunks):
+        turned = [shifted(chunks[t], "dp", lambda i, t=t: along_z(i, t)) for t in range(1, nz)]
+        return [chunks[0]] + turned
+
+    (p_own, q_own), got_q = gather_chips(both, sent_q, send)
 
     owner = own_ids // rows
     before = (owner[:, None] == owner[None, :]) & (number[None, :] < number[:, None])

time: 198 us -> 208 us (1.051)
  starting transfers between devices: 82.9 us -> 98.4 us
  waiting for transfers between devices: 38.7 us -> 32.4 us
    all_to_all x4, starting transfers between devices: 29.1 us -> 37.9 us  [exchange(): lax.all_to_all(value, axis, split_axis=0, concat_axis=0, tiled=True, axis...]
    ppermute x13, starting transfers between devices: 53.7 us -> 60.5 us  [shifted(): return lax.ppermute(value, axis, [(i, move(i)) for i in range(devices)])]
    ppermute x13, waiting for transfers between devices: 22.3 us -> 16 us  [shifted(): return lax.ppermute(value, axis, [(i, move(i)) for i in range(devices)])]
    unnamed x31 -> x29, local copies, waits for them, and re-layouts: 12.6 us -> 12.6 us
  transfers between devices with their start and end apart: 18 -> 18, of which waited for: 8 -> 8; matrix products, arithmetic and copies ran while one was open for 11% -> 10% of each run, Pallas kernels for 10% -> 10%
where the time goes in v3:
time: 208 us; the launch traced here: 206 us
  starting transfers between devices  98.4 us (47%)
  waiting for transfers between devices  32.4 us (16%)
  Pallas kernels  31.2 us (15%)
  local copies, waits for them, and re-layouts  19.2 us (9%)
  between operations  15 us (7%)
  other arithmetic  9.98 us (5%)
    ppermute x13, starting transfers between devices, shifted(): return lax.ppermute(value, axis, [(i, move(i)) for i in range(devices)])  60.5 us
    all_to_all x4, starting transfers between devices, exchange(): lax.all_to_all(value, axis, split_axis=0, concat_axis=0, tiled=True, axis...  37.9 us
    ppermute x13, waiting for transfers between devices, shifted(): return lax.ppermute(value, axis, [(i, move(i)) for i in range(devices)])  16 us
    unnamed x29, local copies, waits for them, and re-layouts  12.6 us
    pallas_call x2, Pallas kernels, grads_of(): pl.pallas_call(grad_kernel, in_specs=[whole] * len(operands) + [pl.BlockS...  11.1 us
    all_to_all x4, waiting for transfers between devices, exchange(): lax.all_to_all(value, axis, split_axis=0, concat_axis=0, tiled=True, axis...  10.2 us
    pallas_call x2, Pallas kernels, exp_scores_of(): pl.pallas_call(exp_kernel, out_shape=(jax.ShapeDtypeStruct((rows, 2 * own...  9.66 us
    all_gather x1, waiting for transfers between devices, local(): lax.all_gather(q_half, 'dp', axis=0, tiled=True, axis_index_groups=lines)  6.22 us
  transfers between devices with their start and end apart: 18, of which 8 were waited for; matrix products, arithmetic and copies ran while one was open for 10% of the time, Pallas kernels for 10%

profile of v3, /device:TPU:2, one launch (start us, length us, event | category | flops | bytes accessed | tf_op | source)
XLA Modules:
  0.0 206.5 jit_solution(17413431680115112560)
XLA Ops:
  7.2 2.2 %unit_halves.1 = (bf16[128,1024]{1,0:T(8,128)(2,1)}, bf16[128,1024]{1,0:T(8,128)(2,1)}, bf16[2,128,1024]{2,1,0:T(8,128)(2,1)}, f32[128,1]{1,0:T(8,128)}, f32[128,1]{1,0:T(8,128)}) custom-call(bf16[128,1024]{1,0:T(8,128)(2,1)} %x_ref.2, bf16[128,1024]{1,0:T(8,128)(2,1)} %x_ref.3), custom_call_target="tpu_custom_call" | custom-call | flops 1048576 | bytes 1572864 | tf_op jit(solution)/shard_map/unit_halves/pallas_call | solution.py:31
  9.4 6.1 %collective-permute-start.2 = (bf16[128,1024]{1,0:T(8,128)(2,1)}, bf16[128,1024]{1,0:T(8,128)(2,1)S(1)}, u32[]{:S(2)}, u32[]{:S(2)}) collective-permute-start(bf16[128,1024]{1,0:T(8,128)(2,1)} %get-tuple-element.42.x_ref), channel_id=1, source_target_pairs={{0,8},{1,9},{2,10},{3,11},{4,12},{5,13},{6,14},{7,15},{8,16},{9,17... | collective-permute-start | bytes 786440 | tf_op jit(solution)/shard_map/ppermute | solution.py:229
  15.5 9.1 %collective-permute-start.1 = (bf16[128,1024]{1,0:T(8,128)(2,1)}, bf16[128,1024]{1,0:T(8,128)(2,1)S(1)}, u32[]{:S(2)}, u32[]{:S(2)}) collective-permute-start(bf16[128,1024]{1,0:T(8,128)(2,1)} %get-tuple-element.42.x_ref), channel_id=1, source_target_pairs={{0,16},{1,17},{2,18},{3,19},{4,20},{5,21},{6,22},{7,23},{8,24},{9,... | collective-permute-start | bytes 786440 | tf_op jit(solution)/shard_map/ppermute | solution.py:229
  24.7 3.7 %collective-permute-start = (bf16[128,1024]{1,0:T(8,128)(2,1)}, bf16[128,1024]{1,0:T(8,128)(2,1)S(1)}, u32[]{:S(2)}, u32[]{:S(2)}) collective-permute-start(bf16[128,1024]{1,0:T(8,128)(2,1)} %get-tuple-element.42.x_ref), channel_id=1, source_target_pairs={{0,24},{1,25},{2,26},{3,27},{4,28},{5,29},{6,30},{7,31},{8,0},{9,1... | collective-permute-start | bytes 786440 | tf_op jit(solution)/shard_map/ppermute | solution.py:229
  28.3 1.3 broadcast_in_dim.129
  29.6 7.1 %all-to-all-start = ((s32[8,1,512]{2,1,0:T(1,128)}), s32[8,1,512]{2,1,0:T(1,128)S(1)}, u32[]{:S(2)}, u32[]{:S(2)}) async-start(s32[8,1,512]{2,1,0:T(1,128)} %broadcast_in_dim.129), calls=%async_computation | async-start | bytes 32768 | tf_op jit(solution)/shard_map/all_to_all | solution.py:222
  36.7 3.4 %collective-permute-start.3 = (bf16[2,128,1024]{2,1,0:T(8,128)(2,1)}, bf16[2,128,1024]{2,1,0:T(8,128)(2,1)S(1)}, u32[]{:S(2)}, u32[]{:S(2)}) collective-permute-start(bf16[2,128,1024]{2,1,0:T(8,128)(2,1)} %get-tuple-element.44), channel_id=1, source_target_pairs={{0,256},{32,288},{64,320},{96,352},{128,384},{160,416},{192,448},{... | collective-permute-start | bytes 1572872 | tf_op jit(solution)/shard_map/ppermute | solution.py:229
  40.1 0.7 add_select_fusion.4
  41.0 3.7 %all-to-all-done = s32[8,1,512]{2,1,0:T(1,128)S(1)} async-done(((s32[8,1,512]{2,1,0:T(1,128)}), s32[8,1,512]{2,1,0:T(1,128)S(1)}, u32[]{:S(2)}, u32[]{:S(2)}) %all-to-all-start) | async-done | bytes 16416 | tf_op jit(solution)/shard_map/all_to_all | solution.py:222
  44.9 0.6 select_reduce_fusion.1
  45.7 3.0 %collective-permute-done = bf16[128,1024]{1,0:T(8,128)(2,1)S(1)} collective-permute-done((bf16[128,1024]{1,0:T(8,128)(2,1)}, bf16[128,1024]{1,0:T(8,128)(2,1)S(1)}, u32[]{:S(2)}, u32[]{:S(2)}) %collective-permute-start) | collective-permute-done | bytes 262176 | tf_op jit(solution)/shard_map/ppermute | solution.py:229
  48.7 1.1 pad_maximum_fusion.pool_ref
  49.8 2.6 %pick_rows.2 = bf16[8,4,32,1024]{3,2,1,0:T(8,128)(2,1)} custom-call(s32[4,1,256]{2,1,0:T(1,128)S(1)} %fusion.19.index_ref, bf16[4,128,1024]{2,1,0:T(8,128)(2,1)S(1)} %pad_maximum_fusion.pool_ref), custom_call_target="tpu_custom_call" | custom-call | flops 268435456 | bytes 3145728 | tf_op jit(solution)/shard_map/pick_rows/pallas_call | solution.py:65
  52.5 6.2 %all-gather.2.cloned.1.call-done = bf16[1024,1024]{1,0:T(8,128)(2,1)} async-done(((bf16[128,1024]{1,0:T(8,128)(2,1)}), bf16[1024,1024]{1,0:T(8,128)(2,1)}) %all-gather.2.cloned.1.call-update) | async-done | bytes 2097168 | tf_op jit(solution)/shard_map/all_gather | solution.py:292
  58.8 1.6 copy-done
  60.4 2.1 pick_rows.3
  62.4 0.8 copy-done.1
  63.2 1.2 pad_maximum_fusion.1
  64.4 3.4 %collective-permute-start.4 = (bf16[2,2,128,1024]{3,2,1,0:T(8,128)(2,1)}, bf16[2,2,128,1024]{3,2,1,0:T(8,128)(2,1)}, u32[]{:S(2)}, u32[]{:S(2)}) collective-permute-start(bf16[2,2,128,1024]{3,2,1,0:T(8,128)(2,1)} %pad_maximum_fusion.1), channel_id=1, source_target_pairs={{0,64},{32,96},{64,128},{96,160},{128,192},{160,224},{192,0},{224,... | collective-permute-start | bytes 3145736 | tf_op jit(solution)/shard_map/ppermute | solution.py:229
  67.8 2.4 %collective-permute-start.5 = (bf16[2,2,128,1024]{3,2,1,0:T(8,128)(2,1)}, bf16[2,2,128,1024]{3,2,1,0:T(8,128)(2,1)S(1)}, u32[]{:S(2)}, u32[]{:S(2)}) collective-permute-start(bf16[2,2,128,1024]{3,2,1,0:T(8,128)(2,1)} %pad_maximum_fusion.1), channel_id=1, source_target_pairs={{0,192},{32,224},{64,0},{96,32},{128,64},{160,96},{192,128},{224,1... | collective-permute-start | bytes 3145736 | tf_op jit(solution)/shard_map/ppermute | solution.py:229
  70.6 0.3 select_reduce_fusion
  70.8 4.8 %collective-permute-start.6 = (bf16[256,1024]{1,0:T(8,128)(2,1)S(1)}, bf16[256,1024]{1,0:T(8,128)(2,1)}, u32[]{:S(2)}, u32[]{:S(2)}) collective-permute-start(bf16[256,1024]{1,0:T(8,128)(2,1)S(1)} %bitcast.177), channel_id=1, source_target_pairs={{0,8},{1,9},{2,10},{3,11},{4,12},{5,13},{6,14},{7,15},{8,16},{9,17... | collective-permute-start | bytes 1572872 | tf_op jit(solution)/shard_map/ppermute | solution.py:229
  75.7 0.4 fusion
  76.1 0.9 convert_element_type.35.mask_ref
  77.0 0.9 bitcast_dynamic-update-slice_fusion.5
  77.8 4.5 %all-to-all-start.1 = ((bf16[8,128,1024]{2,1,0:T(8,128)(2,1)}), bf16[8,128,1024]{2,1,0:T(8,128)(2,1)}, u32[]{:S(2)}, u32[]{:S(2)}) async-start(bf16[8,128,1024]{2,1,0:T(8,128)(2,1)} %bitcast.8), calls=%async_computation.1 | async-start | bytes 4194304 | tf_op jit(solution)/shard_map/all_to_all | solution.py:222
  82.3 6.1 %collective-permute-start.10 = (bf16[256,1024]{1,0:T(8,128)(2,1)S(1)}, bf16[256,1024]{1,0:T(8,128)(2,1)S(1)}, u32[]{:S(2)}, u32[]{:S(2)}) collective-permute-start(bf16[256,1024]{1,0:T(8,128)(2,1)S(1)} %bitcast.176), channel_id=1, source_target_pairs={{0,16},{1,17},{2,18},{3,19},{4,20},{5,21},{6,22},{7,23},{8,24},{9,... | collective-permute-start | bytes 1572872 | tf_op jit(solution)/shard_map/ppermute | solution.py:229
  88.4 5.5 %collective-permute-start.11 = (bf16[256,1024]{1,0:T(8,128)(2,1)S(1)}, bf16[256,1024]{1,0:T(8,128)(2,1)S(1)}, u32[]{:S(2)}, u32[]{:S(2)}) collective-permute-start(bf16[256,1024]{1,0:T(8,128)(2,1)S(1)} %bitcast.175), channel_id=1, source_target_pairs={{0,24},{1,25},{2,26},{3,27},{4,28},{5,29},{6,30},{7,31},{8,0},{9,1... | collective-permute-start | bytes 1572872 | tf_op jit(solution)/shard_map/ppermute | solution.py:229
  93.9 0.8 bitcast_dynamic-update-slice_fusion.4
  94.8 1.9 collective-permute-done.6.rest_1_
  96.7 1.1 slice_bitcast_fusion.1
  97.8 4.1 %collective-permute-start.7 = (bf16[2,128,1024]{2,1,0:T(8,128)(2,1)S(1)}, bf16[2,128,1024]{2,1,0:T(8,128)(2,1)S(1)}, u32[]{:S(2)}, u32[]{:S(2)}) collective-permute-start(bf16[2,128,1024]{2,1,0:T(8,128)(2,1)S(1)} %slice_bitcast_fusion.1), channel_id=1, source_target_pairs={{0,64},{32,96},{64,128},{96,160},{128,192},{160,224},{192,0},{224,... | collective-permute-start | bytes 1572872 | tf_op jit(solution)/shard_map/ppermute | solution.py:229
  101.9 8.1 %collective-permute-start.8 = (bf16[2,128,1024]{2,1,0:T(8,128)(2,1)S(1)}, bf16[2,128,1024]{2,1,0:T(8,128)(2,1)S(1)}, u32[]{:S(2)}, u32[]{:S(2)}) collective-permute-start(bf16[2,128,1024]{2,1,0:T(8,128)(2,1)S(1)} %slice_bitcast_fusion), channel_id=1, source_target_pairs={{0,192},{32,224},{64,0},{96,32},{128,64},{160,96},{192,128},{224,1... | collective-permute-start | bytes 1572872 | tf_op jit(solution)/shard_map/ppermute | solution.py:229
  110.0 1.9 bitcast_dynamic-update-slice_fusion.3
  111.9 1.9 bitcast_dynamic-update-slice_fusion.2
  113.8 1.4 collective-permute-done.7
  115.2 0.8 fusion.5
  116.1 1.2 collective-permute-done.8
  117.3 0.9 fusion.4
  118.1 0.8 bitcast_dynamic-update-slice_fusion.1
  119.0 0.8 bitcast_dynamic-update-slice_fusion
  119.8 1.9 collective-permute-start.9
  121.7 8.5 %collective-permute-done.11.rest_3_ = bf16[256,1024]{1,0:T(8,128)(2,1)S(1)} collective-permute-done((bf16[256,1024]{1,0:T(8,128)(2,1)S(1)}, bf16[256,1024]{1,0:T(8,128)(2,1)S(1)}, u32[]{:S(2)}, u32[]{:S(2)}) %collective-permute-start.11) | collective-permute-done | bytes 524320 | tf_op jit(solution)/shard_map/ppermute | solution.py:229
  130.2 0.8 copy-done.7
  131.0 1.9 collective-permute-start.12
  133.5 0.8 copy.13.mark_ref
  134.5 0.6 iota_add_fusion.mark_ref
  135.2 0.7 iota_add_fusion.1
  136.0 1.4 copy-done.2
  137.4 4.9 %exp_scores.2 = (f32[128,2048]{1,0:T(8,128)}, f32[128,1]{1,0:T(8,128)}) custom-call(bf16[128,1024]{1,0:T(8,128)(2,1)} %get-tuple-element.41.x_ref.q_ref, bf16[1024,1024]{1,0:T(8,128)(2,1)} %get-tuple-element.56.own_ref.own, bf16[1024,1024]{1,0:T(8,128)(2,1)} %copy-done.2), custom_call_target="tpu_custom_call" | custom-call | flops 536870912 | bytes 5505024 | tf_op jit(solution)/shard_map/exp_scores/pallas_call | solution.py:112
  142.2 3.5 %totals.1 = (f32[128,1]{1,0:T(8,128)}, bf16[128,1024]{1,0:T(8,128)(2,1)}, f32[1,1024]{1,0:T(1,128)}, f32[16,2,128]{2,1,0:T(2,128)}) custom-call(bf16[128,1024]{1,0:T(8,128)(2,1)} %get-tuple-element.41.x_ref.q_ref, bf16[1024,1024]{1,0:T(8,128)(2,1)} %bitcast.9.hard_ref.rest_0_, f32[128,1024]{1,0:T(8,128)} %convert_element_type.35.mask_ref, ...), custom_call_target="tpu_custom_call" | custom-call | flops 268435456 | bytes 2883584 | tf_op jit(solution)/shard_map/totals/pallas_call | solution.py:150
  145.8 5.0 %all-to-all-start.2 = ((f32[16,2,128]{2,1,0:T(2,128)}), f32[16,2,128]{2,1,0:T(2,128)S(1)}, u32[]{:S(2)}, u32[]{:S(2)}) async-start(f32[16,2,128]{2,1,0:T(2,128)} %get-tuple-element.62), calls=%async_computation.2 | async-start | bytes 32768 | tf_op jit(solution)/shard_map/all_to_all | solution.py:222
  150.7 0.5 broadcast.610
  151.2 1.3 reduce.3
  152.7 0.3 select_reduce_fusion.2
  152.9 4.8 %exp_scores.3 = (f32[128,2048]{1,0:T(8,128)}, f32[128,1]{1,0:T(8,128)}) custom-call(bf16[128,1024]{1,0:T(8,128)(2,1)} %get-tuple-element.42.x_ref, bf16[1024,1024]{1,0:T(8,128)(2,1)} %get-tuple-element.60.own_ref.own, bf16[1024,1024]{1,0:T(8,128)(2,1)} %collective-permute-done.12.other_ref.other), custom_call_target="tpu_custom_call" | custom-call | flops 536870912 | bytes 5505024 | tf_op jit(solution)/shard_map/exp_scores/pallas_call | solution.py:112
  157.7 0.6 gather_fusion
  158.3 0.6 fusion.18
  158.9 0.6 copy.14
  159.6 21.3 %all-to-all-start.3 = ((f32[32,2,32]{2,1,0:T(2,128)}), f32[32,2,32]{2,1,0:T(2,128)S(1)}, u32[]{:S(2)}, u32[]{:S(2)}) async-start(f32[32,2,32]{2,1,0:T(2,128)} %copy.14), calls=%async_computation.3 | async-start | bytes 65536 | tf_op jit(solution)/shard_map/all_to_all | solution.py:222
  180.9 5.6 %gradients.2 = bf16[128,1024]{1,0:T(8,128)(2,1)} custom-call(f32[128,2048]{1,0:T(8,128)} %get-tuple-element.67.exp_ref, f32[128,1]{1,0:T(8,128)} %get-tuple-element.68.total_ref, s32[128,1]{1,0:T(8,128)} %copy.13.mark_ref, s32[1,2048]{1,0:T(1,128)} %bitcast.187, bf16[1024,1024]{1,0:T(8,128)(2,1)} %get-tuple-element.56.own_ref.own, ...), custom_call_target="tpu_custom_call" | custom-call | flops 805306368 | bytes 8126464 | tf_op jit(solution)/shard_map/gradients/pallas_call | solution.py:202
  186.5 6.5 %all-to-all-done.3 = f32[32,2,32]{2,1,0:T(2,128)S(1)} async-done(((f32[32,2,32]{2,1,0:T(2,128)}), f32[32,2,32]{2,1,0:T(2,128)S(1)}, u32[]{:S(2)}, u32[]{:S(2)}) %all-to-all-start.3) | async-done | bytes 8224 | tf_op jit(solution)/shard_map/all_to_all | solution.py:222
  193.3 0.8 select_convert_fusion.w_ref
  194.1 5.5 %gradients.3 = bf16[128,1024]{1,0:T(8,128)(2,1)} custom-call(f32[128,2048]{1,0:T(8,128)} %get-tuple-element.72.exp_ref, f32[1,2048]{1,0:T(1,128)} %get-tuple-element.97.total_ref, s32[128,1]{1,0:T(8,128)} %iota_add_fusion.mark_ref, s32[1,2048]{1,0:T(1,128)} %get-tuple-element.96.marks_ref, bf16[1024,1024]{1,0:T(8,128)(2,1)} %get-tuple-element.60.own_ref.own, ...), custom_call_target="tpu_custom_call" | custom-call | flops 805306368 | bytes 8126464 | tf_op jit(solution)/shard_map/gradients/pallas_call | solution.py:202
  (63 shorter events, 1.8 us)
Async XLA Ops:
  7.2 51.6 %all-gather.2.cloned.1.call-start = ((), (), s32[]{:S(2)}) async-start(), calls=%async_computation.4 | async-start | bytes 2359296 | tf_op jit(solution)/shard_map/all_gather | solution.py:292
  9.4 36.2 %collective-permute-start.2 = (bf16[128,1024]{1,0:T(8,128)(2,1)}, bf16[128,1024]{1,0:T(8,128)(2,1)S(1)}, u32[]{:S(2)}, u32[]{:S(2)}) collective-permute-start(bf16[128,1024]{1,0:T(8,128)(2,1)} %get-tuple-element.42.x_ref), channel_id=1, source_target_pairs={{0,8},{1,9},{2,10},{3,11},{4,12},{5,13},{6,14},{7,15},{8,16},{9,17... | collective-permute-start | bytes 786440 | tf_op jit(solution)/shard_map/ppermute | solution.py:229
  15.5 30.2 %collective-permute-start.1 = (bf16[128,1024]{1,0:T(8,128)(2,1)}, bf16[128,1024]{1,0:T(8,128)(2,1)S(1)}, u32[]{:S(2)}, u32[]{:S(2)}) collective-permute-start(bf16[128,1024]{1,0:T(8,128)(2,1)} %get-tuple-element.42.x_ref), channel_id=1, source_target_pairs={{0,16},{1,17},{2,18},{3,19},{4,20},{5,21},{6,22},{7,23},{8,24},{9,... | collective-permute-start | bytes 786440 | tf_op jit(solution)/shard_map/ppermute | solution.py:229
  24.7 24.0 %collective-permute-start = (bf16[128,1024]{1,0:T(8,128)(2,1)}, bf16[128,1024]{1,0:T(8,128)(2,1)S(1)}, u32[]{:S(2)}, u32[]{:S(2)}) collective-permute-start(bf16[128,1024]{1,0:T(8,128)(2,1)} %get-tuple-element.42.x_ref), channel_id=1, source_target_pairs={{0,24},{1,25},{2,26},{3,27},{4,28},{5,29},{6,30},{7,31},{8,0},{9,1... | collective-permute-start | bytes 786440 | tf_op jit(solution)/shard_map/ppermute | solution.py:229
  29.6 15.0 %all-to-all-start = ((s32[8,1,512]{2,1,0:T(1,128)}), s32[8,1,512]{2,1,0:T(1,128)S(1)}, u32[]{:S(2)}, u32[]{:S(2)}) async-start(s32[8,1,512]{2,1,0:T(1,128)} %broadcast_in_dim.129), calls=%async_computation | async-start | bytes 32768 | tf_op jit(solution)/shard_map/all_to_all | solution.py:222
  36.7 26.5 %collective-permute-start.3 = (bf16[2,128,1024]{2,1,0:T(8,128)(2,1)}, bf16[2,128,1024]{2,1,0:T(8,128)(2,1)S(1)}, u32[]{:S(2)}, u32[]{:S(2)}) collective-permute-start(bf16[2,128,1024]{2,1,0:T(8,128)(2,1)} %get-tuple-element.44), channel_id=1, source_target_pairs={{0,256},{32,288},{64,320},{96,352},{128,384},{160,416},{192,448},{... | collective-permute-start | bytes 1572872 | tf_op jit(solution)/shard_map/ppermute | solution.py:229
  49.8 13.4 %copy-start.3 = (bf16[2,128,1024]{2,1,0:T(8,128)(2,1)S(1)}, bf16[2,128,1024]{2,1,0:T(8,128)(2,1)}, u32[]{:S(2)}) copy-start(bf16[2,128,1024]{2,1,0:T(8,128)(2,1)} %get-tuple-element.44) | copy-start | bytes 1572868
  58.8 1.6 copy-start
  60.4 10.2 %copy-start.8 = (s32[128,4]{0,1:T(4,128)S(1)}, s32[128,4]{0,1:T(4,128)}, u32[]{:S(2)}) copy-start(s32[128,4]{0,1:T(4,128)} %param.8) | copy-start | bytes 6148
  60.4 10.2 %copy-start.10 = (s32[128]{0:T(128)S(1)}, s32[128]{0:T(128)}, u32[]{:S(2)}) copy-start(s32[128]{0:T(128)} %param.9) | copy-start | bytes 1540
  62.4 0.8 copy-start.1
  63.2 1.2 copy-start.4
  64.4 32.3 %collective-permute-start.4 = (bf16[2,2,128,1024]{3,2,1,0:T(8,128)(2,1)}, bf16[2,2,128,1024]{3,2,1,0:T(8,128)(2,1)}, u32[]{:S(2)}, u32[]{:S(2)}) collective-permute-start(bf16[2,2,128,1024]{3,2,1,0:T(8,128)(2,1)} %pad_maximum_fusion.1), channel_id=1, source_target_pairs={{0,64},{32,96},{64,128},{96,160},{128,192},{160,224},{192,0},{224,... | collective-permute-start | bytes 3145736 | tf_op jit(solution)/shard_map/ppermute | solution.py:229
  67.8 28.9 %collective-permute-start.5 = (bf16[2,2,128,1024]{3,2,1,0:T(8,128)(2,1)}, bf16[2,2,128,1024]{3,2,1,0:T(8,128)(2,1)S(1)}, u32[]{:S(2)}, u32[]{:S(2)}) collective-permute-start(bf16[2,2,128,1024]{3,2,1,0:T(8,128)(2,1)} %pad_maximum_fusion.1), channel_id=1, source_target_pairs={{0,192},{32,224},{64,0},{96,32},{128,64},{160,96},{192,128},{224,1... | collective-permute-start | bytes 3145736 | tf_op jit(solution)/shard_map/ppermute | solution.py:229
  70.8 25.8 %collective-permute-start.6 = (bf16[256,1024]{1,0:T(8,128)(2,1)S(1)}, bf16[256,1024]{1,0:T(8,128)(2,1)}, u32[]{:S(2)}, u32[]{:S(2)}) collective-permute-start(bf16[256,1024]{1,0:T(8,128)(2,1)S(1)} %bitcast.177), channel_id=1, source_target_pairs={{0,8},{1,9},{2,10},{3,11},{4,12},{5,13},{6,14},{7,15},{8,16},{9,17... | collective-permute-start | bytes 1572872 | tf_op jit(solution)/shard_map/ppermute | solution.py:229
  77.8 16.1 %copy-start.5 = (bf16[2,128,1024]{2,1,0:T(8,128)(2,1)S(1)}, bf16[2,128,1024]{2,1,0:T(8,128)(2,1)}, u32[]{:S(2)}) copy-start(bf16[2,128,1024]{2,1,0:T(8,128)(2,1)} %copy-done.4) | copy-start | bytes 1572868
  77.8 64.4 %all-to-all-start.1 = ((bf16[8,128,1024]{2,1,0:T(8,128)(2,1)}), bf16[8,128,1024]{2,1,0:T(8,128)(2,1)}, u32[]{:S(2)}, u32[]{:S(2)}) async-start(bf16[8,128,1024]{2,1,0:T(8,128)(2,1)} %bitcast.8), calls=%async_computation.1 | async-start | bytes 4194304 | tf_op jit(solution)/shard_map/all_to_all | solution.py:222
  82.3 39.4 %collective-permute-start.10 = (bf16[256,1024]{1,0:T(8,128)(2,1)S(1)}, bf16[256,1024]{1,0:T(8,128)(2,1)S(1)}, u32[]{:S(2)}, u32[]{:S(2)}) collective-permute-start(bf16[256,1024]{1,0:T(8,128)(2,1)S(1)} %bitcast.176), channel_id=1, source_target_pairs={{0,16},{1,17},{2,18},{3,19},{4,20},{5,21},{6,22},{7,23},{8,24},{9,... | collective-permute-start | bytes 1572872 | tf_op jit(solution)/shard_map/ppermute | solution.py:229
  88.4 41.8 %collective-permute-start.11 = (bf16[256,1024]{1,0:T(8,128)(2,1)S(1)}, bf16[256,1024]{1,0:T(8,128)(2,1)S(1)}, u32[]{:S(2)}, u32[]{:S(2)}) collective-permute-start(bf16[256,1024]{1,0:T(8,128)(2,1)S(1)} %bitcast.175), channel_id=1, source_target_pairs={{0,24},{1,25},{2,26},{3,27},{4,28},{5,29},{6,30},{7,31},{8,0},{9,1... | collective-permute-start | bytes 1572872 | tf_op jit(solution)/shard_map/ppermute | solution.py:229
  97.8 17.4 %collective-permute-start.7 = (bf16[2,128,1024]{2,1,0:T(8,128)(2,1)S(1)}, bf16[2,128,1024]{2,1,0:T(8,128)(2,1)S(1)}, u32[]{:S(2)}, u32[]{:S(2)}) collective-permute-start(bf16[2,128,1024]{2,1,0:T(8,128)(2,1)S(1)} %slice_bitcast_fusion.1), channel_id=1, source_target_pairs={{0,64},{32,96},{64,128},{96,160},{128,192},{160,224},{192,0},{224,... | collective-permute-start | bytes 1572872 | tf_op jit(solution)/shard_map/ppermute | solution.py:229
  101.9 15.3 %collective-permute-start.8 = (bf16[2,128,1024]{2,1,0:T(8,128)(2,1)S(1)}, bf16[2,128,1024]{2,1,0:T(8,128)(2,1)S(1)}, u32[]{:S(2)}, u32[]{:S(2)}) collective-permute-start(bf16[2,128,1024]{2,1,0:T(8,128)(2,1)S(1)} %slice_bitcast_fusion), channel_id=1, source_target_pairs={{0,192},{32,224},{64,0},{96,32},{128,64},{160,96},{192,128},{224,1... | collective-permute-start | bytes 1572872 | tf_op jit(solution)/shard_map/ppermute | solution.py:229
  116.0 17.4 %copy-start.9 = (s32[128]{0:T(128)S(1)}, s32[128]{0:T(128)}, u32[]{:S(2)}) copy-start(s32[128]{0:T(128)} %param.7) | copy-start | bytes 1540
  119.8 16.2 %collective-permute-start.9 = (bf16[1024,1024]{1,0:T(8,128)(2,1)}, bf16[1024,1024]{1,0:T(8,128)(2,1)S(1)}, u32[]{:S(2)}, u32[]{:S(2)}) collective-permute-start(bf16[1024,1024]{1,0:T(8,128)(2,1)} %get-tuple-element.56.own_ref.own), channel_id=1, source_target_pairs={{0,32},{32,0},{64,96},{96,64},{128,160},{160,128},{192,224},{224,1... | collective-permute-start | bytes 6291464 | tf_op jit(solution)/shard_map/ppermute | solution.py:229
  121.7 8.5 %copy-start.6 = (bf16[256,1024]{1,0:T(8,128)(2,1)}, bf16[256,1024]{1,0:T(8,128)(2,1)S(1)}, u32[]{:S(2)}) copy-start(bf16[256,1024]{1,0:T(8,128)(2,1)S(1)} %collective-permute-done.10.rest_2_) | copy-start | bytes 1572868
  130.2 0.8 copy-start.7
  131.0 11.2 %collective-permute-start.12 = (bf16[1024,1024]{1,0:T(8,128)(2,1)}, bf16[1024,1024]{1,0:T(8,128)(2,1)}, u32[]{:S(2)}, u32[]{:S(2)}) collective-permute-start(bf16[1024,1024]{1,0:T(8,128)(2,1)} %get-tuple-element.60.own_ref.own), channel_id=1, source_target_pairs={{0,32},{32,0},{64,96},{96,64},{128,160},{160,128},{192,224},{224,1... | collective-permute-start | bytes 6291464 | tf_op jit(solution)/shard_map/ppermute | solution.py:229
  136.0 1.4 copy-start.2
  145.8 12.0 %all-to-all-start.2 = ((f32[16,2,128]{2,1,0:T(2,128)}), f32[16,2,128]{2,1,0:T(2,128)S(1)}, u32[]{:S(2)}, u32[]{:S(2)}) async-start(f32[16,2,128]{2,1,0:T(2,128)} %get-tuple-element.62), calls=%async_computation.2 | async-start | bytes 32768 | tf_op jit(solution)/shard_map/all_to_all | solution.py:222
  159.6 33.4 %all-to-all-start.3 = ((f32[32,2,32]{2,1,0:T(2,128)}), f32[32,2,32]{2,1,0:T(2,128)S(1)}, u32[]{:S(2)}, u32[]{:S(2)}) async-start(f32[32,2,32]{2,1,0:T(2,128)} %copy.14), calls=%async_computation.3 | async-start | bytes 65536 | tf_op jit(solution)/shard_map/all_to_all | solution.py:222
Sparse Core Ops, SparseCore 0:
  10.7 48.0 all-gather.1
